TPU v7x, 256 devices: a whole 4x4x8 slice. The times are simulated.
256 devices in a mesh: gx: 16 (over y_hi, z), gy: 16 (over y_lo, x, core).
Axes of the slice: x: 4, y: 4 (y_hi: 2, y_lo: 2; y = y_hi * 2 + y_lo), z: 8, core: 2. Of those that a mesh axis runs over, the one named last changes fastest.
Arguments:
- velocity: float32 [3, 6, 512, 2048], P(None, None, 'gx', 'gy'), may hold values from -6 to 6
- stress: float32 [6, 6, 512, 2048], P(None, None, 'gx', 'gy'), may hold values from -6 to 6
- lame_first: float32 [6, 512, 2048], P(None, 'gx', 'gy'), may hold values from 0.3 to 1
- shear: float32 [6, 512, 2048], P(None, 'gx', 'gy'), may hold values from 0.2 to 0.6
- buoyancy: float32 [6, 512, 2048], P(None, 'gx', 'gy'), may hold values from 0.5 to 1.5
- fwd_strain: bfloat16 [6, 6, 512, 2048], P(None, None, 'gx', 'gy'), may hold values from -6 to 6
- fwd_accel: bfloat16 [3, 6, 512, 2048], P(None, None, 'gx', 'gy'), may hold values from -6 to 6
- kernels: float32 [3, 6, 512, 2048], P(None, None, 'gx', 'gy'), may hold values from -6 to 6
- station_trace: float32 [131072, 6], P(('gx', 'gy')), may hold values from -6 to 6
- station_tile: int32 [131072, 1], P(('gx', 'gy')), may hold values from 0 to 255; in each aligned block of 512 rows (0 to 511, 512 to 1023, ...) at most 4 rows name the same one
- station_cell: int32 [131072], P(('gx', 'gy')), may hold values from 0 to 24575
- station_count: int32 [256], P(('gx', 'gy')), may hold values from 1 to 512, 98304 in all
Outputs:
- velocity_out: float32 [3, 6, 512, 2048], P(None, None, 'gx', 'gy')
- stress_out: float32 [6, 6, 512, 2048], P(None, None, 'gx', 'gy')
- kernels_out: float32 [3, 6, 512, 2048], P(None, None, 'gx', 'gy')
Inputs may be any that keep to these rules, and one draw needn't show every extreme that they name: `station_tile`: in each device's block of 512 rows no tile is named by more than 4 rows, and every tile is named somewhere.
All inputs are finite; a program needn't handle non-finite values. No bound on the sum of `station_count` on one device may be relied on, other than what follows from the above.
Results may differ from a plain program's by a relative error of at most 0.0003.
Values sent between devices are 32-bit elements; how exact they have to be, the bound alone decides.
A program may use at most 192 MiB of HBM per device.

v0:
```python
import jax
import jax.numpy as jnp
from jax import lax
from jax.sharding import PartitionSpec as P

STEPS = 2
CAP = 4


C_NEAR = 9.0 / 8.0
C_FAR = -1.0 / 24.0
STEP_DT = 0.25


def padded_2(cells, sides, width):
    for axis, dim in sides:
        count = lax.axis_size(axis)
        ends = count - 1
        head = lax.slice_in_dim(cells, 0, width, axis=dim)
        tail = lax.slice_in_dim(cells, cells.shape[dim] - width, cells.shape[dim], axis=dim)
        cells = jnp.concatenate(
            [
                lax.ppermute(tail, axis, [(i, (i + 1) % count) for i in range(ends)]),
                cells,
                lax.ppermute(head, axis, [((i + 1) % count, i) for i in range(ends)]),
            ],
            axis=dim,
        )
    return cells


def stencil(padded, axis, upward):
    count = padded.shape[axis] - 4

    def take(offset):
        return lax.slice_in_dim(padded, 2 + offset, 2 + offset + count, axis=axis)

    if upward:
        return C_NEAR * (take(1) - take(0)) + C_FAR * (take(2) - take(-1))
    return C_NEAR * (take(0) - take(-1)) + C_FAR * (take(1) - take(-2))


def derive(field, axis, upward):
    widths = [(0, 0)] * field.ndim
    widths[axis] = (2, 2)
    return stencil(jnp.pad(field, widths), axis, upward)


def body(
    velocity,
    stress,
    lame_first,
    shear,
    buoyancy,
    fwd_strain,
    fwd_accel,
    kernels,
    station_trace,
    station_tile,
    station_cell,
    station_count,
):
    depth, width_x, width_y = (velocity.shape[1], velocity.shape[2], velocity.shape[3])
    cells = depth * width_x * width_y
    rows = station_trace.shape[0]
    samples = station_trace.shape[1]
    count_x = lax.axis_size("gx")
    count_y = lax.axis_size("gy")
    tiles = count_x * count_y
    live = jnp.arange(rows, dtype=jnp.int32) < station_count[0]
    values = jnp.where(live[:, None], station_trace, jnp.zeros_like(station_trace))
    target = station_tile[:, 0]
    onehot = (target[:, None] == jnp.arange(tiles, dtype=jnp.int32)[None, :]).astype(jnp.int32)
    before = jnp.cumsum(onehot, axis=0) - onehot
    slot = jnp.sum(before * onehot, axis=1)
    dest = target * CAP + slot
    payload = jnp.concatenate([values, station_cell.astype(jnp.float32)[:, None]], axis=1)
    packed = jnp.zeros((tiles * CAP, samples + 1), jnp.float32).at[dest].set(payload)
    packed = packed.reshape(count_x, count_y, CAP, samples + 1)
    arrived = lax.all_to_all(
        lax.all_to_all(packed, "gx", split_axis=0, concat_axis=0, tiled=True),
        "gy",
        split_axis=1,
        concat_axis=1,
        tiled=True,
    )
    arrived = arrived.reshape(tiles * CAP, samples + 1)
    amounts = arrived[:, :samples]
    spots = arrived[:, samples].astype(jnp.int32)
    sources = jnp.zeros((samples, cells), jnp.float32).at[:, spots].add(amounts.T)
    sources = sources.reshape(samples // 3, 3, depth, width_x, width_y)
    speed = velocity
    tension = stress
    for step in range(STEPS):
        whole = padded_2(tension, (("gx", 2), ("gy", 3)), 2)
        along_x = whole[:, :, :, 2:-2]
        along_y = whole[:, :, 2:-2, :]
        sxx_x, sxz_x, sxy_x = (along_x[0], along_x[1], along_x[2])
        sxy_y, syy_y, syz_y = (along_y[2], along_y[3], along_y[4])
        rate_x = stencil(sxx_x, 1, True) + stencil(sxy_y, 2, False) + derive(tension[1], 0, False)
        rate_y = stencil(sxy_x, 1, False) + stencil(syy_y, 2, True) + derive(tension[4], 0, False)
        rate_z = stencil(sxz_x, 1, False) + stencil(syz_y, 2, False) + derive(tension[5], 0, True)
        source = sources[step]
        vx = speed[0] + STEP_DT * buoyancy * (rate_x + source[0])
        vy = speed[1] + STEP_DT * buoyancy * (rate_y + source[1])
        vz = speed[2] + STEP_DT * buoyancy * (rate_z + source[2])
        speed = jnp.stack([vx, vy, vz])
        framed = padded_2(speed, (("gx", 2), ("gy", 3)), 2)
        speed_x = framed[:, :, :, 2:-2]
        speed_y = framed[:, :, 2:-2, :]
        exx = stencil(speed_x[0], 1, False)
        eyy = stencil(speed_y[1], 2, False)
        ezz = derive(vz, 0, False)
        gxy = stencil(speed_y[0], 2, True) + stencil(speed_x[1], 1, True)
        gxz = derive(vx, 0, True) + stencil(speed_x[2], 1, True)
        gyz = derive(vy, 0, True) + stencil(speed_y[2], 2, True)
        spread = exx + eyy + ezz
        sxx = tension[0] + STEP_DT * (lame_first * spread + 2.0 * shear * exx)
        syy = tension[3] + STEP_DT * (lame_first * spread + 2.0 * shear * eyy)
        szz = tension[5] + STEP_DT * (lame_first * spread + 2.0 * shear * ezz)
        sxy = tension[2] + STEP_DT * shear * gxy
        sxz = tension[1] + STEP_DT * shear * gxz
        syz = tension[4] + STEP_DT * shear * gyz
        tension = jnp.stack([sxx, sxz, sxy, syy, syz, szz])
    strain = fwd_strain.astype(jnp.float32)
    accel = fwd_accel.astype(jnp.float32)
    kernel_lame = kernels[0] - STEP_DT * (strain[0] + strain[3] + strain[5]) * spread
    kernel_shear = kernels[1] - 2.0 * STEP_DT * (
        strain[0] * exx
        + strain[3] * eyy
        + strain[5] * ezz
        + strain[2] * gxy
        + strain[1] * gxz
        + strain[4] * gyz
    )
    kernel_mass = kernels[2] - STEP_DT * (
        accel[0] * speed[0] + accel[1] * speed[1] + accel[2] * speed[2]
    )
    return (speed, tension, jnp.stack([kernel_lame, kernel_shear, kernel_mass]))


def solution(mesh):
    return jax.shard_map(
        body,
        mesh=mesh,
        in_specs=(
            P(None, None, "gx", "gy"),
            P(None, None, "gx", "gy"),
            P(None, "gx", "gy"),
            P(None, "gx", "gy"),
            P(None, "gx", "gy"),
            P(None, None, "gx", "gy"),
            P(None, None, "gx", "gy"),
            P(None, None, "gx", "gy"),
            P(("gx", "gy"), None),
            P(("gx", "gy"), None),
            P(("gx", "gy")),
            P(("gx", "gy")),
        ),
        out_specs=(P(None, None, "gx", "gy"), P(None, None, "gx", "gy"), P(None, None, "gx", "gy")),
        check_vma=False,
    )
```

profile of v0, /device:TPU:24, one launch (start us, length us, event | category | flops | bytes accessed | tf_op | source)
XLA Modules:
  0.0 204.0 jit_solution(13531260760315371372)
XLA Ops:
  0.6 0.9 copy.30
  1.9 0.9 fusion.3
  5.8 1.8 scatter_custom_fusion
  8.1 0.8 reshape.79
  8.9 11.4 %all-to-all-start = ((f32[16,1,448]{2,1,0:T(1,128)}), f32[16,1,448]{2,1,0:T(1,128)S(1)}, u32[]{:S(2)}, u32[]{:S(2)}) async-start(f32[16,1,448]{2,1,0:T(1,128)} %reshape.79), calls=%async_computation | async-start | bytes 65536 | tf_op jit(solution)/shard_map/all_to_all | solution.py:81
  20.4 1.0 fusion.225
  21.4 4.6 %collective-permute-start.1 = (f32[6,6,2,128]{3,2,1,0:T(2,128)S(1)}, f32[6,6,2,128]{3,2,1,0:T(2,128)S(1)}, u32[]{:S(2)}, u32[]{:S(2)}) collective-permute-start(f32[6,6,2,128]{3,2,1,0:T(2,128)S(1)} %get-tuple-element.62), channel_id=1, source_target_pairs={{16,0},{32,16},{48,32},{64,48},{80,64},{96,80},{112,96},{128,112},... | collective-permute-start | bytes 110600 | tf_op jit(solution)/shard_map/ppermute | solution.py:25
  26.0 1.9 collective-permute-start
  27.9 1.7 slice_bitcast_fusion.16
  29.6 5.9 %collective-permute-done = f32[6,6,2,128]{3,2,1,0:T(2,128)S(1)} collective-permute-done((f32[6,6,2,128]{3,2,1,0:T(2,128)S(1)}, f32[6,6,2,128]{3,2,1,0:T(2,128)S(1)}, u32[]{:S(2)}, u32[]{:S(2)}) %collective-permute-start) | collective-permute-done | bytes 36896 | tf_op jit(solution)/shard_map/ppermute | solution.py:23
  35.5 1.1 pad_maximum_fusion
  37.2 2.3 %collective-permute-start.3 = (f32[6,6,36,2]{2,3,1,0:T(2,128)S(1)}, f32[6,6,36,2]{2,3,1,0:T(2,128)S(1)}, u32[]{:S(2)}, u32[]{:S(2)}) collective-permute-start(f32[6,6,36,2]{2,3,1,0:T(2,128)S(1)} %copy.27), channel_id=1, source_target_pairs={{1,0},{2,1},{3,2},{4,3},{5,4},{6,5},{7,6},{8,7},{9,8},{10,9},{11,1... | collective-permute-start | bytes 31112 | tf_op jit(solution)/shard_map/ppermute | solution.py:25
  39.8 2.0 collective-permute-start.2
  41.9 1.0 maximum_bitcast_fusion.12
  43.3 3.9 %collective-permute-done.2 = f32[6,6,36,2]{2,3,1,0:T(2,128)S(1)} collective-permute-done((f32[6,6,36,2]{2,3,1,0:T(2,128)S(1)}, f32[6,6,36,2]{2,3,1,0:T(2,128)S(1)}, u32[]{:S(2)}, u32[]{:S(2)}) %collective-permute-start.2) | collective-permute-done | bytes 10400 | tf_op jit(solution)/shard_map/ppermute | solution.py:23
  49.2 0.8 reshape.81
  50.0 3.4 %all-to-all-start.1 = ((f32[16,1,448]{2,1,0:T(1,128)}), f32[16,1,448]{2,1,0:T(1,128)S(1)}, u32[]{:S(2)}, u32[]{:S(2)}) async-start(f32[16,1,448]{2,1,0:T(1,128)} %reshape.81), calls=%async_computation.1 | async-start | bytes 65536 | tf_op jit(solution)/shard_map/all_to_all | solution.py:80
  53.7 4.3 %all-to-all-done.1 = f32[16,1,448]{2,1,0:T(1,128)S(1)} async-done(((f32[16,1,448]{2,1,0:T(1,128)}), f32[16,1,448]{2,1,0:T(1,128)S(1)}, u32[]{:S(2)}, u32[]{:S(2)}) %all-to-all-start.1) | async-done | bytes 28704 | tf_op jit(solution)/shard_map/all_to_all | solution.py:80
  60.5 11.3 %scatter_custom_fusion.1 = f32[6,24576]{0,1:T(8,128)} fusion(s32[1024]{0:T(1024)S(1)} %bitcast.280, f32[1024,6]{1,0:T(8,128)S(1)} %copy.36, f32[]{:T(128)} %constant.13.clone.1), kind=kCustom, calls=%fused_computation.8 | custom fusion | flops 6144 | bytes 589828 | tf_op jit(solution)/shard_map/scatter-add | solution.py:90
  71.8 49.0 %slice_reduce_fusion.2 = (f32[24576]{0:T(1024)}, f32[24576]{0:T(1024)}, f32[24576]{0:T(1024)}, f32[24576]{0:T(1024)S(1)}, f32[24576]{0:T(1024)S(1)}, /*index=5*/f32[24576]{0:T(1024)S(1)}) fusion(f32[6,24576]{0,1:T(8,128)} %scatter_custom_fusion.1), kind=kLoop, calls=%fused_computation.4 | loop fusion | bytes 1179648 | tf_op jit(solution)/shard_map/slice | solution.py:104
  121.3 3.2 %collective-permute-start.5 = (f32[3,6,2,128]{3,2,1,0:T(2,128)S(1)}, f32[3,6,2,128]{3,2,1,0:T(2,128)S(1)}, u32[]{:S(2)}, u32[]{:S(2)}) collective-permute-start(f32[3,6,2,128]{3,2,1,0:T(2,128)S(1)} %get-tuple-element.76), channel_id=1, source_target_pairs={{16,0},{32,16},{48,32},{64,48},{80,64},{96,80},{112,96},{128,112},... | collective-permute-start | bytes 55304 | tf_op jit(solution)/shard_map/ppermute | solution.py:25
  124.5 2.7 %collective-permute-start.4 = (f32[3,6,2,128]{3,2,1,0:T(2,128)S(1)}, f32[3,6,2,128]{3,2,1,0:T(2,128)S(1)}, u32[]{:S(2)}, u32[]{:S(2)}) collective-permute-start(f32[3,6,2,128]{3,2,1,0:T(2,128)S(1)} %get-tuple-element.75), channel_id=1, source_target_pairs={{0,16},{16,32},{32,48},{48,64},{64,80},{80,96},{96,112},{112,128},... | collective-permute-start | bytes 55304 | tf_op jit(solution)/shard_map/ppermute | solution.py:23
  127.2 6.6 %collective-permute-done.4 = f32[3,6,2,128]{3,2,1,0:T(2,128)S(1)} collective-permute-done((f32[3,6,2,128]{3,2,1,0:T(2,128)S(1)}, f32[3,6,2,128]{3,2,1,0:T(2,128)S(1)}, u32[]{:S(2)}, u32[]{:S(2)}) %collective-permute-start.4) | collective-permute-done | bytes 18464 | tf_op jit(solution)/shard_map/ppermute | solution.py:23
  134.0 1.9 collective-permute-start.7
  135.9 2.4 %collective-permute-start.6 = (f32[3,6,36,2]{3,2,1,0:T(8,128)S(1)}, f32[3,6,36,2]{3,2,1,0:T(8,128)S(1)}, u32[]{:S(2)}, u32[]{:S(2)}) collective-permute-start(f32[3,6,36,2]{3,2,1,0:T(8,128)S(1)} %get-tuple-element.71), channel_id=1, source_target_pairs={{0,1},{1,2},{2,3},{3,4},{4,5},{5,6},{6,7},{7,8},{8,9},{9,10},{10,1... | collective-permute-start | bytes 15560 | tf_op jit(solution)/shard_map/ppermute | solution.py:23
  138.4 2.6 %collective-permute-done.7 = f32[3,6,36,2]{3,2,1,0:T(8,128)S(1)} collective-permute-done((f32[3,6,36,2]{3,2,1,0:T(8,128)S(1)}, f32[3,6,36,2]{3,2,1,0:T(8,128)S(1)}, u32[]{:S(2)}, u32[]{:S(2)}) %collective-permute-start.7) | collective-permute-done | bytes 5216 | tf_op jit(solution)/shard_map/ppermute | solution.py:25
  140.9 5.9 %collective-permute-done.6 = f32[3,6,36,2]{3,2,1,0:T(8,128)S(1)} collective-permute-done((f32[3,6,36,2]{3,2,1,0:T(8,128)S(1)}, f32[3,6,36,2]{3,2,1,0:T(8,128)S(1)}, u32[]{:S(2)}, u32[]{:S(2)}) %collective-permute-start.6) | collective-permute-done | bytes 5216 | tf_op jit(solution)/shard_map/ppermute | solution.py:23
  148.7 0.8 bitcast_dynamic-update-slice_fusion.9
  149.6 0.8 bitcast_dynamic-update-slice_fusion.7
  151.1 2.3 %collective-permute-start.9 = (f32[6,6,2,128]{3,2,1,0:T(2,128)S(1)}, f32[6,6,2,128]{3,2,1,0:T(2,128)S(1)}, u32[]{:S(2)}, u32[]{:S(2)}) collective-permute-start(f32[6,6,2,128]{3,2,1,0:T(2,128)S(1)} %get-tuple-element.57), channel_id=1, source_target_pairs={{16,0},{32,16},{48,32},{64,48},{80,64},{96,80},{112,96},{128,112},... | collective-permute-start | bytes 110600 | tf_op jit(solution)/shard_map/ppermute | solution.py:25
  153.4 3.6 %collective-permute-start.8 = (f32[6,6,2,128]{3,2,1,0:T(2,128)S(1)}, f32[6,6,2,128]{3,2,1,0:T(2,128)S(1)}, u32[]{:S(2)}, u32[]{:S(2)}) collective-permute-start(f32[6,6,2,128]{3,2,1,0:T(2,128)S(1)} %get-tuple-element.56), channel_id=1, source_target_pairs={{0,16},{16,32},{32,48},{48,64},{64,80},{80,96},{96,112},{112,128},... | collective-permute-start | bytes 110600 | tf_op jit(solution)/shard_map/ppermute | solution.py:23
  157.0 0.7 convert_element_type.38
  157.7 5.1 %collective-permute-done.8 = f32[6,6,2,128]{3,2,1,0:T(2,128)S(1)} collective-permute-done((f32[6,6,2,128]{3,2,1,0:T(2,128)S(1)}, f32[6,6,2,128]{3,2,1,0:T(2,128)S(1)}, u32[]{:S(2)}, u32[]{:S(2)}) %collective-permute-start.8) | collective-permute-done | bytes 36896 | tf_op jit(solution)/shard_map/ppermute | solution.py:23
  163.5 1.9 collective-permute-start.11
  165.8 2.4 %collective-permute-start.10 = (f32[6,6,36,2]{2,3,1,0:T(2,128)S(1)}, f32[6,6,36,2]{2,3,1,0:T(2,128)}, u32[]{:S(2)}, u32[]{:S(2)}) collective-permute-start(f32[6,6,36,2]{2,3,1,0:T(2,128)S(1)} %copy.37), channel_id=1, source_target_pairs={{0,1},{1,2},{2,3},{3,4},{4,5},{5,6},{6,7},{7,8},{8,9},{9,10},{10,1... | collective-permute-start | bytes 31112 | tf_op jit(solution)/shard_map/ppermute | solution.py:23
  168.7 4.6 %collective-permute-done.10 = f32[6,6,36,2]{2,3,1,0:T(2,128)} collective-permute-done((f32[6,6,36,2]{2,3,1,0:T(2,128)S(1)}, f32[6,6,36,2]{2,3,1,0:T(2,128)}, u32[]{:S(2)}, u32[]{:S(2)}) %collective-permute-start.10) | collective-permute-done | bytes 10400 | tf_op jit(solution)/shard_map/ppermute | solution.py:23
  173.3 1.1 copy.39
  174.5 1.1 fusion.10
  175.6 1.9 fusion.109
  177.6 1.9 collective-permute-start.13
  179.5 3.9 %collective-permute-start.12 = (f32[3,6,2,128]{3,2,1,0:T(2,128)S(1)}, f32[3,6,2,128]{3,2,1,0:T(2,128)S(1)}, u32[]{:S(2)}, u32[]{:S(2)}) collective-permute-start(f32[3,6,2,128]{3,2,1,0:T(2,128)S(1)} %get-tuple-element.73), channel_id=1, source_target_pairs={{0,16},{16,32},{32,48},{48,64},{64,80},{80,96},{96,112},{112,128},... | collective-permute-start | bytes 55304 | tf_op jit(solution)/shard_map/ppermute | solution.py:23
  183.5 1.0 convert_element_type.37
  184.5 4.3 %collective-permute-done.12 = f32[3,6,2,128]{3,2,1,0:T(2,128)S(1)} collective-permute-done((f32[3,6,2,128]{3,2,1,0:T(2,128)S(1)}, f32[3,6,2,128]{3,2,1,0:T(2,128)S(1)}, u32[]{:S(2)}, u32[]{:S(2)}) %collective-permute-start.12) | collective-permute-done | bytes 18464 | tf_op jit(solution)/shard_map/ppermute | solution.py:23
  189.0 1.9 collective-permute-start.15
  191.0 2.4 %collective-permute-start.14 = (f32[3,6,36,2]{3,2,1,0:T(8,128)S(1)}, f32[3,6,36,2]{3,2,1,0:T(8,128)S(1)}, u32[]{:S(2)}, u32[]{:S(2)}) collective-permute-start(f32[3,6,36,2]{3,2,1,0:T(8,128)S(1)} %get-tuple-element.66), channel_id=1, source_target_pairs={{0,1},{1,2},{2,3},{3,4},{4,5},{5,6},{6,7},{7,8},{8,9},{9,10},{10,1... | collective-permute-start | bytes 15560 | tf_op jit(solution)/shard_map/ppermute | solution.py:23
  193.4 2.6 %collective-permute-done.15 = f32[3,6,36,2]{3,2,1,0:T(8,128)S(1)} collective-permute-done((f32[3,6,36,2]{3,2,1,0:T(8,128)S(1)}, f32[3,6,36,2]{3,2,1,0:T(8,128)S(1)}, u32[]{:S(2)}, u32[]{:S(2)}) %collective-permute-start.15) | collective-permute-done | bytes 5216 | tf_op jit(solution)/shard_map/ppermute | solution.py:25
  196.0 5.9 %collective-permute-done.14 = f32[3,6,36,2]{3,2,1,0:T(8,128)S(1)} collective-permute-done((f32[3,6,36,2]{3,2,1,0:T(8,128)S(1)}, f32[3,6,36,2]{3,2,1,0:T(8,128)S(1)}, u32[]{:S(2)}, u32[]{:S(2)}) %collective-permute-start.14) | collective-permute-done | bytes 5216 | tf_op jit(solution)/shard_map/ppermute | solution.py:23
  203.1 0.8 pad_maximum_fusion.5
  (112 shorter events, 15.5 us)
Async XLA Ops:
  0.6 52.8 %copy-start = (f32[6,6,32,128]{3,2,1,0:T(8,128)S(1)}, f32[6,6,32,128]{3,2,1,0:T(8,128)}, u32[]{:S(2)}) copy-start(f32[6,6,32,128]{3,2,1,0:T(8,128)} %param.13) | copy-start | bytes 1769476
  8.9 38.7 %all-to-all-start = ((f32[16,1,448]{2,1,0:T(1,128)}), f32[16,1,448]{2,1,0:T(1,128)S(1)}, u32[]{:S(2)}, u32[]{:S(2)}) async-start(f32[16,1,448]{2,1,0:T(1,128)} %reshape.79), calls=%async_computation | async-start | bytes 65536 | tf_op jit(solution)/shard_map/all_to_all | solution.py:81
  21.4 8.2 %collective-permute-start.1 = (f32[6,6,2,128]{3,2,1,0:T(2,128)S(1)}, f32[6,6,2,128]{3,2,1,0:T(2,128)S(1)}, u32[]{:S(2)}, u32[]{:S(2)}) collective-permute-start(f32[6,6,2,128]{3,2,1,0:T(2,128)S(1)} %get-tuple-element.62), channel_id=1, source_target_pairs={{16,0},{32,16},{48,32},{64,48},{80,64},{96,80},{112,96},{128,112},... | collective-permute-start | bytes 110600 | tf_op jit(solution)/shard_map/ppermute | solution.py:25
  26.0 9.5 %collective-permute-start = (f32[6,6,2,128]{3,2,1,0:T(2,128)S(1)}, f32[6,6,2,128]{3,2,1,0:T(2,128)S(1)}, u32[]{:S(2)}, u32[]{:S(2)}) collective-permute-start(f32[6,6,2,128]{3,2,1,0:T(2,128)S(1)} %get-tuple-element.61), channel_id=1, source_target_pairs={{0,16},{16,32},{32,48},{48,64},{64,80},{80,96},{96,112},{112,128},... | collective-permute-start | bytes 110600 | tf_op jit(solution)/shard_map/ppermute | solution.py:23
  37.2 5.7 %collective-permute-start.3 = (f32[6,6,36,2]{2,3,1,0:T(2,128)S(1)}, f32[6,6,36,2]{2,3,1,0:T(2,128)S(1)}, u32[]{:S(2)}, u32[]{:S(2)}) collective-permute-start(f32[6,6,36,2]{2,3,1,0:T(2,128)S(1)} %copy.27), channel_id=1, source_target_pairs={{1,0},{2,1},{3,2},{4,3},{5,4},{6,5},{7,6},{8,7},{9,8},{10,9},{11,1... | collective-permute-start | bytes 31112 | tf_op jit(solution)/shard_map/ppermute | solution.py:25
  39.8 7.4 %collective-permute-start.2 = (f32[6,6,36,2]{2,3,1,0:T(2,128)S(1)}, f32[6,6,36,2]{2,3,1,0:T(2,128)S(1)}, u32[]{:S(2)}, u32[]{:S(2)}) collective-permute-start(f32[6,6,36,2]{2,3,1,0:T(2,128)S(1)} %copy.26), channel_id=1, source_target_pairs={{0,1},{1,2},{2,3},{3,4},{4,5},{5,6},{6,7},{7,8},{8,9},{9,10},{10,1... | collective-permute-start | bytes 31112 | tf_op jit(solution)/shard_map/ppermute | solution.py:23
  50.0 8.1 %all-to-all-start.1 = ((f32[16,1,448]{2,1,0:T(1,128)}), f32[16,1,448]{2,1,0:T(1,128)S(1)}, u32[]{:S(2)}, u32[]{:S(2)}) async-start(f32[16,1,448]{2,1,0:T(1,128)} %reshape.81), calls=%async_computation.1 | async-start | bytes 65536 | tf_op jit(solution)/shard_map/all_to_all | solution.py:80
  71.8 49.0 %copy-start.2 = (f32[6,32,128]{2,1,0:T(8,128)S(1)}, f32[6,32,128]{2,1,0:T(8,128)}, u32[]{:S(2)}) copy-start(f32[6,32,128]{2,1,0:T(8,128)} %param.16) | copy-start | bytes 294916
  71.8 49.0 %copy-start.9 = (f32[6,32,128]{2,1,0:T(8,128)S(1)}, f32[6,32,128]{2,1,0:T(8,128)}, u32[]{:S(2)}) copy-start(f32[6,32,128]{2,1,0:T(8,128)} %get-tuple-element.60) | copy-start | bytes 294916
  71.8 49.0 %copy-start.16 = (f32[3,6,32,128]{3,2,1,0:T(8,128)S(1)}, f32[3,6,32,128]{3,2,1,0:T(8,128)}, u32[]{:S(2)}) copy-start(f32[3,6,32,128]{3,2,1,0:T(8,128)} %param.12) | copy-start | bytes 884740
  71.8 49.2 %copy-start.8 = (f32[6,32,128]{2,1,0:T(8,128)S(1)}, f32[6,32,128]{2,1,0:T(8,128)}, u32[]{:S(2)}) copy-start(f32[6,32,128]{2,1,0:T(8,128)} %get-tuple-element.59) | copy-start | bytes 294916
  71.8 75.2 %copy-start.1 = (f32[6,32,128]{2,1,0:T(8,128)S(1)}, f32[6,32,128]{2,1,0:T(8,128)}, u32[]{:S(2)}) copy-start(f32[6,32,128]{2,1,0:T(8,128)} %param.15) | copy-start | bytes 294916
  71.8 75.2 %copy-start.11 = (f32[6,32,128]{2,1,0:T(8,128)S(1)}, f32[6,32,128]{2,1,0:T(8,128)}, u32[]{:S(2)}) copy-start(f32[6,32,128]{2,1,0:T(8,128)} %param.14) | copy-start | bytes 294916
  120.8 36.2 %copy-start.18 = (bf16[3,6,32,128]{3,2,1,0:T(8,128)(2,1)S(1)}, bf16[3,6,32,128]{3,2,1,0:T(8,128)(2,1)}, u32[]{:S(2)}) copy-start(bf16[3,6,32,128]{3,2,1,0:T(8,128)(2,1)} %param.18) | copy-start | bytes 442372
  121.3 5.9 %collective-permute-start.5 = (f32[3,6,2,128]{3,2,1,0:T(2,128)S(1)}, f32[3,6,2,128]{3,2,1,0:T(2,128)S(1)}, u32[]{:S(2)}, u32[]{:S(2)}) collective-permute-start(f32[3,6,2,128]{3,2,1,0:T(2,128)S(1)} %get-tuple-element.76), channel_id=1, source_target_pairs={{16,0},{32,16},{48,32},{64,48},{80,64},{96,80},{112,96},{128,112},... | collective-permute-start | bytes 55304 | tf_op jit(solution)/shard_map/ppermute | solution.py:25
  124.5 9.3 %collective-permute-start.4 = (f32[3,6,2,128]{3,2,1,0:T(2,128)S(1)}, f32[3,6,2,128]{3,2,1,0:T(2,128)S(1)}, u32[]{:S(2)}, u32[]{:S(2)}) collective-permute-start(f32[3,6,2,128]{3,2,1,0:T(2,128)S(1)} %get-tuple-element.75), channel_id=1, source_target_pairs={{0,16},{16,32},{32,48},{48,64},{64,80},{80,96},{96,112},{112,128},... | collective-permute-start | bytes 55304 | tf_op jit(solution)/shard_map/ppermute | solution.py:23
  134.0 6.9 %collective-permute-start.7 = (f32[3,6,36,2]{3,2,1,0:T(8,128)S(1)}, f32[3,6,36,2]{3,2,1,0:T(8,128)S(1)}, u32[]{:S(2)}, u32[]{:S(2)}) collective-permute-start(f32[3,6,36,2]{3,2,1,0:T(8,128)S(1)} %get-tuple-element.72), channel_id=1, source_target_pairs={{1,0},{2,1},{3,2},{4,3},{5,4},{6,5},{7,6},{8,7},{9,8},{10,9},{11,1... | collective-permute-start | bytes 15560 | tf_op jit(solution)/shard_map/ppermute | solution.py:25
  135.9 10.9 %collective-permute-start.6 = (f32[3,6,36,2]{3,2,1,0:T(8,128)S(1)}, f32[3,6,36,2]{3,2,1,0:T(8,128)S(1)}, u32[]{:S(2)}, u32[]{:S(2)}) collective-permute-start(f32[3,6,36,2]{3,2,1,0:T(8,128)S(1)} %get-tuple-element.71), channel_id=1, source_target_pairs={{0,1},{1,2},{2,3},{3,4},{4,5},{5,6},{6,7},{7,8},{8,9},{9,10},{10,1... | collective-permute-start | bytes 15560 | tf_op jit(solution)/shard_map/ppermute | solution.py:23
  147.8 15.1 %copy-start.3 = (f32[6,32,128]{2,1,0:T(8,128)}, f32[6,32,128]{2,1,0:T(8,128)S(1)}, u32[]{:S(2)}) copy-start(f32[6,32,128]{2,1,0:T(8,128)S(1)} %get-tuple-element.33) | copy-start | bytes 294916
  151.1 6.6 %collective-permute-start.9 = (f32[6,6,2,128]{3,2,1,0:T(2,128)S(1)}, f32[6,6,2,128]{3,2,1,0:T(2,128)S(1)}, u32[]{:S(2)}, u32[]{:S(2)}) collective-permute-start(f32[6,6,2,128]{3,2,1,0:T(2,128)S(1)} %get-tuple-element.57), channel_id=1, source_target_pairs={{16,0},{32,16},{48,32},{64,48},{80,64},{96,80},{112,96},{128,112},... | collective-permute-start | bytes 110600 | tf_op jit(solution)/shard_map/ppermute | solution.py:25
  153.4 9.5 %collective-permute-start.8 = (f32[6,6,2,128]{3,2,1,0:T(2,128)S(1)}, f32[6,6,2,128]{3,2,1,0:T(2,128)S(1)}, u32[]{:S(2)}, u32[]{:S(2)}) collective-permute-start(f32[6,6,2,128]{3,2,1,0:T(2,128)S(1)} %get-tuple-element.56), channel_id=1, source_target_pairs={{0,16},{16,32},{32,48},{48,64},{64,80},{80,96},{96,112},{112,128},... | collective-permute-start | bytes 110600 | tf_op jit(solution)/shard_map/ppermute | solution.py:23
  162.8 5.8 %copy-start.15 = (f32[6,6,2,128]{3,2,1,0:T(2,128)}, f32[6,6,2,128]{3,2,1,0:T(2,128)S(1)}, u32[]{:S(2)}) copy-start(f32[6,6,2,128]{3,2,1,0:T(2,128)S(1)} %collective-permute-done.8) | copy-start | bytes 110596
  163.5 4.7 %collective-permute-start.11 = (f32[6,6,36,2]{2,3,1,0:T(2,128)S(1)}, f32[6,6,36,2]{2,3,1,0:T(2,128)S(1)}, u32[]{:S(2)}, u32[]{:S(2)}) collective-permute-start(f32[6,6,36,2]{2,3,1,0:T(2,128)S(1)} %copy.38), channel_id=1, source_target_pairs={{1,0},{2,1},{3,2},{4,3},{5,4},{6,5},{7,6},{8,7},{9,8},{10,9},{11,1... | collective-permute-start | bytes 31112 | tf_op jit(solution)/shard_map/ppermute | solution.py:25
  165.8 7.5 %collective-permute-start.10 = (f32[6,6,36,2]{2,3,1,0:T(2,128)S(1)}, f32[6,6,36,2]{2,3,1,0:T(2,128)}, u32[]{:S(2)}, u32[]{:S(2)}) collective-permute-start(f32[6,6,36,2]{2,3,1,0:T(2,128)S(1)} %copy.37), channel_id=1, source_target_pairs={{0,1},{1,2},{2,3},{3,4},{4,5},{5,6},{6,7},{7,8},{8,9},{9,10},{10,1... | collective-permute-start | bytes 31112 | tf_op jit(solution)/shard_map/ppermute | solution.py:23
  174.4 27.7 %copy-start.17 = (f32[3,6,32,128]{3,2,1,0:T(8,128)S(1)}, f32[3,6,32,128]{3,2,1,0:T(8,128)}, u32[]{:S(2)}) copy-start(f32[3,6,32,128]{3,2,1,0:T(8,128)} %param.19) | copy-start | bytes 884740
  174.4 27.9 %copy-start.12 = (f32[6,32,128]{2,1,0:T(8,128)S(1)}, f32[6,32,128]{2,1,0:T(8,128)}, u32[]{:S(2)}) copy-start(f32[6,32,128]{2,1,0:T(8,128)} %param.14) | copy-start | bytes 294916
  174.5 27.9 %copy-start.13 = (f32[6,32,128]{2,1,0:T(8,128)S(1)}, f32[6,32,128]{2,1,0:T(8,128)}, u32[]{:S(2)}) copy-start(f32[6,32,128]{2,1,0:T(8,128)} %get-tuple-element.34) | copy-start | bytes 294916
  174.5 28.4 %copy-start.5 = (f32[6,32,128]{2,1,0:T(8,128)S(1)}, f32[6,32,128]{2,1,0:T(8,128)}, u32[]{:S(2)}) copy-start(f32[6,32,128]{2,1,0:T(8,128)} %get-tuple-element.30) | copy-start | bytes 294916
  174.5 28.4 %copy-start.10 = (f32[6,32,128]{2,1,0:T(8,128)S(1)}, f32[6,32,128]{2,1,0:T(8,128)}, u32[]{:S(2)}) copy-start(f32[6,32,128]{2,1,0:T(8,128)} %get-tuple-element.28) | copy-start | bytes 294916
  174.5 28.5 %copy-start.4 = (f32[6,32,128]{2,1,0:T(8,128)S(1)}, f32[6,32,128]{2,1,0:T(8,128)}, u32[]{:S(2)}) copy-start(f32[6,32,128]{2,1,0:T(8,128)} %copy-done.3) | copy-start | bytes 294916
  174.5 28.5 %copy-start.6 = (f32[6,32,128]{2,1,0:T(8,128)S(1)}, f32[6,32,128]{2,1,0:T(8,128)}, u32[]{:S(2)}) copy-start(f32[6,32,128]{2,1,0:T(8,128)} %get-tuple-element.26) | copy-start | bytes 294916
  174.5 28.6 %copy-start.7 = (f32[6,32,128]{2,1,0:T(8,128)S(1)}, f32[6,32,128]{2,1,0:T(8,128)}, u32[]{:S(2)}) copy-start(f32[6,32,128]{2,1,0:T(8,128)} %get-tuple-element.24) | copy-start | bytes 294916
  177.6 26.4 %copy-start.14 = (f32[3,6,32,128]{3,2,1,0:T(8,128)}, f32[3,6,32,128]{3,2,1,0:T(8,128)S(1)}, u32[]{:S(2)}) copy-start(f32[3,6,32,128]{3,2,1,0:T(8,128)S(1)} %pad_maximum_fusion.4) | copy-start | bytes 884740
  177.6 6.9 %collective-permute-start.13 = (f32[3,6,2,128]{3,2,1,0:T(2,128)S(1)}, f32[3,6,2,128]{3,2,1,0:T(2,128)S(1)}, u32[]{:S(2)}, u32[]{:S(2)}) collective-permute-start(f32[3,6,2,128]{3,2,1,0:T(2,128)S(1)} %get-tuple-element.74), channel_id=1, source_target_pairs={{16,0},{32,16},{48,32},{64,48},{80,64},{96,80},{112,96},{128,112},... | collective-permute-start | bytes 55304 | tf_op jit(solution)/shard_map/ppermute | solution.py:25
  179.5 9.3 %collective-permute-start.12 = (f32[3,6,2,128]{3,2,1,0:T(2,128)S(1)}, f32[3,6,2,128]{3,2,1,0:T(2,128)S(1)}, u32[]{:S(2)}, u32[]{:S(2)}) collective-permute-start(f32[3,6,2,128]{3,2,1,0:T(2,128)S(1)} %get-tuple-element.73), channel_id=1, source_target_pairs={{0,16},{16,32},{32,48},{48,64},{64,80},{80,96},{96,112},{112,128},... | collective-permute-start | bytes 55304 | tf_op jit(solution)/shard_map/ppermute | solution.py:23
  189.0 6.9 %collective-permute-start.15 = (f32[3,6,36,2]{3,2,1,0:T(8,128)S(1)}, f32[3,6,36,2]{3,2,1,0:T(8,128)S(1)}, u32[]{:S(2)}, u32[]{:S(2)}) collective-permute-start(f32[3,6,36,2]{3,2,1,0:T(8,128)S(1)} %get-tuple-element.67), channel_id=1, source_target_pairs={{1,0},{2,1},{3,2},{4,3},{5,4},{6,5},{7,6},{8,7},{9,8},{10,9},{11,1... | collective-permute-start | bytes 15560 | tf_op jit(solution)/shard_map/ppermute | solution.py:25
  191.0 10.9 %collective-permute-start.14 = (f32[3,6,36,2]{3,2,1,0:T(8,128)S(1)}, f32[3,6,36,2]{3,2,1,0:T(8,128)S(1)}, u32[]{:S(2)}, u32[]{:S(2)}) collective-permute-start(f32[3,6,36,2]{3,2,1,0:T(8,128)S(1)} %get-tuple-element.66), channel_id=1, source_target_pairs={{0,1},{1,2},{2,3},{3,4},{4,5},{5,6},{6,7},{7,8},{8,9},{9,10},{10,1... | collective-permute-start | bytes 15560 | tf_op jit(solution)/shard_map/ppermute | solution.py:23
  203.1 0.9 copy-start.19
where the time goes:
time: 205 us; the launch traced here: 204 us
  local copies, waits for them, and re-layouts  64 us (31%)
  starting transfers between devices  56.2 us (27%)
  waiting for transfers between devices  51.7 us (25%)
  other arithmetic  30.2 us (15%)
    slice x1, local copies, waits for them, and re-layouts, body(): vx = speed[0] + STEP_DT * buoyancy * (rate_x + source[0])  49 us
    ppermute x8, waiting for transfers between devices, padded_2(): lax.ppermute(tail, axis, [(i, (i + 1) % count) for i in range(ends)])  42.3 us
    ppermute x8, starting transfers between devices, padded_2(): lax.ppermute(tail, axis, [(i, (i + 1) % count) for i in range(ends)])  21.3 us
    ppermute x8, starting transfers between devices, padded_2(): lax.ppermute(head, axis, [((i + 1) % count, i) for i in range(ends)])  20 us
    all_to_all x1, starting transfers between devices, body(): lax.all_to_all(packed, 'gx', split_axis=0, concat_axis=0, tiled=True)  11.4 us
    scatter-add x1, other arithmetic, body(): jnp.zeros((samples, cells), jnp.float32).at[:, spots].add(amounts.T)  11.3 us
    ppermute x8, waiting for transfers between devices, padded_2(): lax.ppermute(head, axis, [((i + 1) % count, i) for i in range(ends)])  5.14 us
    all_to_all x1, waiting for transfers between devices, body(): lax.all_to_all(lax.all_to_all(packed, 'gx', split_axis=0, concat_axis=0,...  4.34 us
  transfers between devices with their start and end apart: 18, of which 11 were waited for; matrix products, arithmetic and copies ran while one was open for 5% of the time, Pallas kernels for 0%

commit v1 on v0

v1 whole, which is shorter than its diff:
```python
import functools

import jax
import jax.numpy as jnp
from jax import lax
from jax.experimental import pallas as pl
from jax.experimental.pallas import tpu as pltpu
from jax.sharding import PartitionSpec as P

STEPS = 2
CAP = 4
C_NEAR = 9.0 / 8.0
C_FAR = -1.0 / 24.0
STEP_DT = 0.25
MESH = pl.DeviceIdType.MESH

LANES = 128
FEATURES = 8
MARGIN = 8
ZPAD = 2
SXX, SXZ, SXY, SYY, SYZ, SZZ = range(6)
STRESS_X = (SXX, SXZ, SXY)
STRESS_Y = (SXY, SYY, SYZ)
SPEED_ALL = (0, 1, 2)
EXCHANGES = 2 * STEPS


def pieces(value):
    high = value.astype(jnp.bfloat16)
    rest = value - high.astype(jnp.float32)
    middle = rest.astype(jnp.bfloat16)
    low = (rest - middle.astype(jnp.float32)).astype(jnp.bfloat16)
    return high, middle, low


def dot_nt(left, right):
    return lax.dot_general(left, right, (((1,), (1,)), ((), ())), preferred_element_type=jnp.float32)


def kernel(
    n_x,
    n_y,
    vel_in,
    str_in,
    lame_in,
    shear_in,
    buoy_in,
    strain_in,
    accel_in,
    kern_in,
    trace_in,
    tile_in,
    cell_in,
    count,
    vel_out,
    str_out,
    kern_out,
    speed,
    tension,
    lame,
    shear,
    buoy,
    strain,
    accel,
    kern,
    trace,
    tile,
    cell,
    source,
    payload,
    packed,
    first_hop,
    second_hop,
    spot_rows,
    spot_cols,
    x_send,
    x_recv,
    y_send,
    y_recv,
    in_sem,
    out_sem,
    hop_send,
    hop_recv,
    face_send,
    face_recv,
):
    depth, width = buoy.shape[0], buoy.shape[1]
    rows = trace.shape[1]
    tiles = n_x * n_y
    gx, gy = lax.axis_index("gx"), lax.axis_index("gy")
    inner = pl.ds(MARGIN, width)
    planes = pl.ds(ZPAD, depth)

    loads = [
        pltpu.make_async_copy(src, dst, in_sem.at[i])
        for i, (src, dst) in enumerate(
            (
                (trace_in, trace),
                (tile_in, tile),
                (cell_in, cell),
                (str_in, tension.at[:, planes, inner, :]),
                (vel_in, speed.at[:, planes, inner, :]),
                (buoy_in, buoy),
                (lame_in, lame),
                (shear_in, shear),
                (strain_in, strain),
                (accel_in, accel),
                (kern_in, kern),
            )
        )
    ]
    for load in loads:
        load.start()

    barrier = pltpu.get_barrier_semaphore()

    def greet_x(i, _):
        pl.semaphore_signal(barrier, inc=1, device_id=(lax.rem(gx + i, n_x), gy), device_id_type=MESH)
        return 0

    def greet_y(i, _):
        pl.semaphore_signal(barrier, inc=1, device_id=(gx, lax.rem(gy + i, n_y)), device_id_type=MESH)
        return 0

    lax.fori_loop(1, n_x, greet_x, 0)
    lax.fori_loop(1, n_y, greet_y, 0)

    blank = jnp.zeros((ZPAD, width, LANES), jnp.float32)
    for ref, comps in ((speed, SPEED_ALL), (tension, (SXZ, SYZ, SZZ))):
        for comp in comps:
            ref[comp, pl.ds(0, ZPAD), inner, :] = blank
            ref[comp, pl.ds(ZPAD + depth, ZPAD), inner, :] = blank

    for load in loads[:3]:
        load.wait()
    names = tile[...]
    line = lax.broadcasted_iota(jnp.int32, (tiles, rows), 0)
    named = (line == names).astype(jnp.float32)
    named_16 = named.astype(jnp.bfloat16)
    earlier = (
        lax.broadcasted_iota(jnp.int32, (rows, rows), 0) < lax.broadcasted_iota(jnp.int32, (rows, rows), 1)
    ).astype(jnp.float32).astype(jnp.bfloat16)
    ahead = jnp.dot(named_16, earlier, preferred_element_type=jnp.float32)
    slot = jnp.sum(named * ahead, axis=0, keepdims=True)
    live = lax.broadcasted_iota(jnp.int32, (1, rows), 1) < count[0]
    cells = cell[...]
    samples = trace.shape[0]
    payload[pl.ds(0, samples), :] = jnp.where(live, trace[...], 0.0)
    payload[pl.ds(samples, 1), :] = (cells // LANES).astype(jnp.float32)
    payload[pl.ds(samples + 1, 1), :] = (cells % LANES).astype(jnp.float32)
    load_all = payload[...]
    parts = [jnp.where(slot == float(s), load_all, 0.0) for s in range(CAP)]
    parts.append(jnp.zeros((LANES - CAP * FEATURES, rows), jnp.float32))
    bundle = jnp.concatenate(parts, axis=0)
    outgoing = sum(dot_nt(named_16, piece) for piece in pieces(bundle))
    packed[...] = outgoing.reshape(n_x, n_y, 1, LANES)

    lane = lax.broadcasted_iota(jnp.int32, (width, LANES), 1)

    def face_copies(phase):
        up_x = (lax.rem(gx + 1, n_x), gy)
        down_x = (lax.rem(gx + n_x - 1, n_x), gy)
        up_y = (gx, lax.rem(gy + 1, n_y))
        down_y = (gx, lax.rem(gy + n_y - 1, n_y))
        return [
            pltpu.make_async_remote_copy(
                src_ref=send.at[phase, side],
                dst_ref=recv.at[phase, side],
                send_sem=face_send.at[phase, k],
                recv_sem=face_recv.at[phase, k],
                device_id=target,
                device_id_type=MESH,
            )
            for k, (send, recv, side, target) in enumerate(
                (
                    (y_send, y_recv, 0, down_y),
                    (y_send, y_recv, 1, up_y),
                    (x_send, x_recv, 0, down_x),
                    (x_send, x_recv, 1, up_x),
                )
            )
        ]

    def pack_faces(phase, ref, comps_x, comps_y):
        for k, comp in enumerate(comps_x):
            def rows_of(z, _, k=k, comp=comp):
                at = k * depth + z
                x_send[phase, 0, at] = ref[comp, z + ZPAD, pl.ds(MARGIN, 2), :]
                x_send[phase, 1, at] = ref[comp, z + ZPAD, pl.ds(MARGIN + width - 2, 2), :]
                return 0

            lax.fori_loop(0, depth, rows_of, 0, unroll=True)
        carried = (jnp.zeros((width, LANES), jnp.float32),) * 2
        for k, comp in enumerate(comps_y):
            def strip(z, carry, k=k, comp=comp):
                start = 2 * (k * depth + z)
                turned = pltpu.roll(ref[comp, z + ZPAD, inner, :], start + 2, 1)
                return (
                    jnp.where(lane >= start + 2, turned, carry[0]),
                    jnp.where(lane >= start, turned, carry[1]),
                )

            carried = lax.fori_loop(0, depth, strip, carried, unroll=True)
        y_send[phase, 0] = carried[0]
        y_send[phase, 1] = carried[1]

    def take_faces(phase, ref, comps_x):
        for copy in face_copies(phase):
            copy.wait_recv()

        @pl.when(gy == n_y - 1)
        def _():
            y_recv[phase, 0] = jnp.zeros((width, LANES), jnp.float32)

        @pl.when(gy == 0)
        def _():
            y_recv[phase, 1] = jnp.zeros((width, LANES), jnp.float32)

        @pl.when(gx == n_x - 1)
        def _():
            x_recv[phase, 0] = jnp.zeros(x_recv.shape[2:], jnp.float32)

        @pl.when(gx == 0)
        def _():
            x_recv[phase, 1] = jnp.zeros(x_recv.shape[2:], jnp.float32)

        for k, comp in enumerate(comps_x):
            def rows_of(z, _, k=k, comp=comp):
                at = k * depth + z
                ref[comp, z + ZPAD, pl.ds(MARGIN + width, 2), :] = x_recv[phase, 0, at]
                ref[comp, z + ZPAD, pl.ds(MARGIN - 2, 2), :] = x_recv[phase, 1, at]
                return 0

            lax.fori_loop(0, depth, rows_of, 0, unroll=True)

    def along_z(ref, comp, z, upward):
        def at(offset):
            return ref[comp, z + ZPAD + offset, inner, :]

        return difference(at, upward)

    def along_x(ref, comp, z, upward):
        def at(offset):
            return ref[comp, z + ZPAD, pl.ds(MARGIN + offset, width), :]

        return difference(at, upward)

    def along_y(phase, ref, comp, k, z, upward):
        start = 2 * (k * depth + z) + 2
        side = jnp.where(lane >= start, y_recv[phase, 0], y_recv[phase, 1])
        side = pltpu.roll(side, LANES - start, 1)
        centre = ref[comp, z + ZPAD, inner, :]

        def at(offset):
            if offset == 0:
                return centre
            if offset > 0:
                return pltpu.roll(jnp.where(lane < offset, side, centre), LANES - offset, 1)
            return pltpu.roll(jnp.where(lane >= LANES + offset, side, centre), -offset, 1)

        return difference(at, upward)

    def difference(at, upward):
        if upward:
            return C_NEAR * (at(1) - at(0)) + C_FAR * (at(2) - at(-1))
        return C_NEAR * (at(0) - at(-1)) + C_FAR * (at(1) - at(-2))

    def push_speed(phase):
        def plane(z, _):
            rate_x = (
                along_x(tension, SXX, z, True)
                + along_y(phase, tension, SXY, 0, z, False)
                + along_z(tension, SXZ, z, False)
            )
            rate_y = (
                along_x(tension, SXY, z, False)
                + along_y(phase, tension, SYY, 1, z, True)
                + along_z(tension, SYZ, z, False)
            )
            rate_z = (
                along_x(tension, SXZ, z, False)
                + along_y(phase, tension, SYZ, 2, z, False)
                + along_z(tension, SZZ, z, True)
            )
            factor = STEP_DT * buoy[z]
            for k, rate in enumerate((rate_x, rate_y, rate_z)):
                if phase > 0:
                    rate = rate + source[3 * (phase // 2) + k, z]
                speed[k, z + ZPAD, inner, :] = speed[k, z + ZPAD, inner, :] + factor * rate
            return 0

        lax.fori_loop(0, depth, plane, 0, unroll=True)

    def add_source(step):
        def plane(z, _):
            factor = STEP_DT * buoy[z]
            for k in range(3):
                speed[k, z + ZPAD, inner, :] = speed[k, z + ZPAD, inner, :] + factor * source[3 * step + k, z]
            return 0

        lax.fori_loop(0, depth, plane, 0, unroll=True)

    def push_stress(phase, last):
        def plane(z, _):
            exx = along_x(speed, 0, z, False)
            eyy = along_y(phase, speed, 1, 1, z, False)
            ezz = along_z(speed, 2, z, False)
            gxy = along_y(phase, speed, 0, 0, z, True) + along_x(speed, 1, z, True)
            gxz = along_z(speed, 0, z, True) + along_x(speed, 2, z, True)
            gyz = along_z(speed, 1, z, True) + along_y(phase, speed, 2, 2, z, True)
            spread = exx + eyy + ezz
            stiff = STEP_DT * shear[z]
            common = STEP_DT * lame[z] * spread
            for comp, change in (
                (SXX, common + 2.0 * stiff * exx),
                (SYY, common + 2.0 * stiff * eyy),
                (SZZ, common + 2.0 * stiff * ezz),
                (SXY, stiff * gxy),
                (SXZ, stiff * gxz),
                (SYZ, stiff * gyz),
            ):
                tension[comp, z + ZPAD, inner, :] = tension[comp, z + ZPAD, inner, :] + change
            if last:
                f = [strain[comp, z].astype(jnp.float32) for comp in range(6)]
                a = [accel[comp, z].astype(jnp.float32) for comp in range(3)]
                v = [speed[comp, z + ZPAD, inner, :] for comp in range(3)]
                kern[0, z] = kern[0, z] - STEP_DT * (f[SXX] + f[SYY] + f[SZZ]) * spread
                kern[1, z] = kern[1, z] - 2.0 * STEP_DT * (
                    f[SXX] * exx + f[SYY] * eyy + f[SZZ] * ezz + f[SXY] * gxy + f[SXZ] * gxz + f[SYZ] * gyz
                )
                kern[2, z] = kern[2, z] - STEP_DT * (a[0] * v[0] + a[1] * v[1] + a[2] * v[2])
            return 0

        lax.fori_loop(0, depth, plane, 0, unroll=True)

    loads[3].wait()
    pack_faces(0, tension, STRESS_X, STRESS_Y)
    pl.semaphore_wait(barrier, n_x + n_y - 2)

    def hop_x(i):
        to = lax.rem(gx + i, n_x)
        return pltpu.make_async_remote_copy(
            src_ref=packed.at[to],
            dst_ref=first_hop.at[:, gx],
            send_sem=hop_send.at[0, i],
            recv_sem=hop_recv.at[0, i],
            device_id=(to, gy),
            device_id_type=MESH,
        )

    def hop_y(i):
        to = lax.rem(gy + i, n_y)
        return pltpu.make_async_remote_copy(
            src_ref=first_hop.at[to],
            dst_ref=second_hop.at[gy],
            send_sem=hop_send.at[1, i],
            recv_sem=hop_recv.at[1, i],
            device_id=(gx, to),
            device_id_type=MESH,
        )

    def start(make):
        def run(i, _):
            make(i).start()
            return 0

        return run

    def landed(make):
        def run(i, _):
            make(i).wait_recv()
            return 0

        return run

    def sent(make):
        def run(i, _):
            make(i).wait_send()
            return 0

        return run

    own_x = pltpu.make_async_copy(packed.at[gx], first_hop.at[:, gx], hop_recv.at[0, 0])
    own_y = pltpu.make_async_copy(first_hop.at[gy], second_hop.at[gy], hop_recv.at[1, 0])
    lax.fori_loop(1, n_x, start(hop_x), 0)
    own_x.start()
    for copy in face_copies(0):
        copy.start()
    own_x.wait()
    lax.fori_loop(1, n_x, landed(hop_x), 0)
    lax.fori_loop(1, n_y, start(hop_y), 0)
    own_y.start()

    take_faces(0, tension, STRESS_X)
    loads[4].wait()
    loads[5].wait()
    push_speed(0)

    own_y.wait()
    lax.fori_loop(1, n_y, landed(hop_y), 0)
    arrived = second_hop[...].reshape(tiles, LANES).T
    row_of = lax.broadcasted_iota(jnp.int32, (depth * width, tiles), 0).astype(jnp.float32)
    col_of = lax.broadcasted_iota(jnp.int32, (LANES, tiles), 0).astype(jnp.float32)
    values = []
    for s in range(CAP):
        group = arrived[s * FEATURES : (s + 1) * FEATURES, :]
        span = pl.ds(s * tiles, tiles)
        spot_rows[:, span] = (row_of == group[samples : samples + 1]).astype(jnp.float32).astype(jnp.bfloat16)
        spot_cols[:, span] = (col_of == group[samples + 1 : samples + 2]).astype(jnp.float32).astype(jnp.bfloat16)
        values.append(group)
    amounts = pieces(jnp.concatenate(values, axis=1))

    def lay_sources(step):
        columns = spot_cols[...]
        total = jnp.zeros((depth * width, 3 * LANES), jnp.float32)
        for amount in amounts:
            spread = [columns * amount[3 * step + k : 3 * step + k + 1, :] for k in range(3)]
            total = total + dot_nt(spot_rows[...], jnp.concatenate(spread, axis=0))
        for k in range(3):
            source[3 * step + k] = total[:, k * LANES : (k + 1) * LANES].reshape(depth, width, LANES)

    lay_sources(0)
    add_source(0)
    for step in range(STEPS):
        phase = 2 * step + 1
        pack_faces(phase, speed, SPEED_ALL, SPEED_ALL)
        for copy in face_copies(phase):
            copy.start()
        if step + 1 < STEPS:
            lay_sources(step + 1)
            loads[6].wait()
            loads[7].wait()
        else:
            out_speed = pltpu.make_async_copy(speed.at[:, planes, inner, :], vel_out, out_sem.at[0])
            out_speed.start()
            for load in loads[8:]:
                load.wait()
        take_faces(phase, speed, SPEED_ALL)
        push_stress(phase, step + 1 == STEPS)
        if step + 1 < STEPS:
            phase = phase + 1
            pack_faces(phase, tension, STRESS_X, STRESS_Y)
            for copy in face_copies(phase):
                copy.start()
            take_faces(phase, tension, STRESS_X)
            push_speed(phase)
    out_rest = [
        pltpu.make_async_copy(tension.at[:, planes, inner, :], str_out, out_sem.at[1]),
        pltpu.make_async_copy(kern, kern_out, out_sem.at[2]),
    ]
    for copy in out_rest:
        copy.start()
    lax.fori_loop(1, n_x, sent(hop_x), 0)
    lax.fori_loop(1, n_y, sent(hop_y), 0)
    for phase in range(EXCHANGES):
        for copy in face_copies(phase):
            copy.wait_send()
    out_speed.wait()
    for copy in out_rest:
        copy.wait()


def body(
    velocity,
    stress,
    lame_first,
    shear,
    buoyancy,
    fwd_strain,
    fwd_accel,
    kernels,
    station_trace,
    station_tile,
    station_cell,
    station_count,
):
    n_x, n_y = lax.axis_size("gx"), lax.axis_size("gy")
    depth, width, lanes = buoyancy.shape
    rows = station_trace.shape[0]
    tiles = n_x * n_y
    strips = 3 * depth
    padded = (depth + 2 * ZPAD, width + 2 * MARGIN, lanes)
    f32, b16 = jnp.float32, jnp.bfloat16
    far = pl.BlockSpec(memory_space=pltpu.HBM)
    return pl.pallas_call(
        functools.partial(kernel, n_x, n_y),
        out_shape=[
            jax.ShapeDtypeStruct(velocity.shape, f32),
            jax.ShapeDtypeStruct(stress.shape, f32),
            jax.ShapeDtypeStruct(kernels.shape, f32),
        ],
        in_specs=[far] * 11 + [pl.BlockSpec(memory_space=pltpu.SMEM)],
        out_specs=[far] * 3,
        scratch_shapes=[
            pltpu.VMEM((3, *padded), f32),
            pltpu.VMEM((6, *padded), f32),
            pltpu.VMEM(buoyancy.shape, f32),
            pltpu.VMEM(buoyancy.shape, f32),
            pltpu.VMEM(buoyancy.shape, f32),
            pltpu.VMEM(fwd_strain.shape, b16),
            pltpu.VMEM(fwd_accel.shape, b16),
            pltpu.VMEM(kernels.shape, f32),
            pltpu.VMEM(station_trace.shape[::-1], f32),
            pltpu.VMEM((1, rows), jnp.int32),
            pltpu.VMEM((1, rows), jnp.int32),
            pltpu.VMEM((3 * STEPS, *buoyancy.shape), f32),
            pltpu.VMEM((FEATURES, rows), f32),
            pltpu.VMEM((n_x, n_y, 1, lanes), f32),
            pltpu.VMEM((n_y, n_x, 1, lanes), f32),
            pltpu.VMEM((n_y, n_x, 1, lanes), f32),
            pltpu.VMEM((depth * width, CAP * tiles), b16),
            pltpu.VMEM((lanes, CAP * tiles), b16),
            pltpu.VMEM((EXCHANGES, 2, strips, 2, lanes), f32),
            pltpu.VMEM((EXCHANGES, 2, strips, 2, lanes), f32),
            pltpu.VMEM((EXCHANGES, 2, width, lanes), f32),
            pltpu.VMEM((EXCHANGES, 2, width, lanes), f32),
            pltpu.SemaphoreType.DMA((11,)),
            pltpu.SemaphoreType.DMA((3,)),
            pltpu.SemaphoreType.DMA((2, max(n_x, n_y))),
            pltpu.SemaphoreType.DMA((2, max(n_x, n_y))),
            pltpu.SemaphoreType.DMA((EXCHANGES, 4)),
            pltpu.SemaphoreType.DMA((EXCHANGES, 4)),
        ],
        compiler_params=pltpu.CompilerParams(
            collective_id=0, has_side_effects=True, vmem_limit_bytes=60 * 1024 * 1024
        ),
    )(
        velocity,
        stress,
        lame_first,
        shear,
        buoyancy,
        fwd_strain,
        fwd_accel,
        kernels,
        station_trace.T,
        station_tile.reshape(1, rows),
        station_cell.reshape(1, rows),
        station_count,
    )


def solution(mesh):
    tiled = P(None, None, "gx", "gy")
    plane = P(None, "gx", "gy")
    listed = ("gx", "gy")
    return jax.shard_map(
        body,
        mesh=mesh,
        in_specs=(
            tiled,
            tiled,
            plane,
            plane,
            plane,
            tiled,
            tiled,
            tiled,
            P(listed, None),
            P(listed, None),
            P(listed),
            P(listed),
        ),
        out_specs=(tiled, tiled, tiled),
        check_vma=False,
    )
```

time: 205 us -> 48.1 us (0.23)
  the two profiles are of different devices: /device:TPU:24 before, /device:TPU:1 now
where the time goes in v1:
time: 48.1 us; the launch traced here: 47.6 us
  Pallas kernels  42.7 us (89%)
  local copies, waits for them, and re-layouts  3.6 us (7%)
  between operations  1.3 us (3%)
    pallas_call x1, Pallas kernels, body(): pl.pallas_call(functools.partial(kernel, n_x, n_y), out_shape=[jax.ShapeD...  42.7 us
    unnamed x7, local copies, waits for them, and re-layouts  3.6 us

profile of v1, /device:TPU:1, one launch (start us, length us, event | category | flops | bytes accessed | tf_op | source)
XLA Modules:
  0.0 47.6 jit_solution(5035475440403573380)
XLA Ops:
  1.3 42.7 %shard_map.139 = (f32[3,6,32,128]{3,2,1,0:T(8,128)}, f32[6,6,32,128]{3,2,1,0:T(8,128)}, f32[3,6,32,128]{3,2,1,0:T(8,128)}) custom-call(f32[3,6,32,128]{3,2,1,0:T(8,128)} %vel_in.1, f32[6,6,32,128]{3,2,1,0:T(8,128)} %str_in.1, f32[6,32,128]{2,1,0:T(8,128)} %lame_in.1, f32[6,32,128]{2,1,0:T(8,128)} %shear_in.1, f32[6,32,128]{2,1,0:T(8,128)} %buoy_in.1, ...), custom_call_target="tpu_custom_call" | custom-call | tf_op jit(solution)/shard_map/pallas_call | solution.py:485
  44.0 0.0 copy-start
  44.0 1.8 %copy.19 = f32[3,6,32,128]{3,2,1,0:T(8,128)} copy(f32[3,6,32,128]{3,2,1,0:T(8,128)} %get-tuple-element.6) | data formatting | bytes 589824
  45.8 0.0 copy-done
  45.8 0.0 copy-start.1
  45.8 0.8 %copy.20 = f32[6,6,32,128]{3,2,1,0:T(8,128)} copy(f32[6,6,32,128]{3,2,1,0:T(8,128)S(1)} %copy-done) | data formatting | bytes 1179648
  46.6 0.3 copy-done.1
  46.9 0.7 %copy.21 = f32[3,6,32,128]{3,2,1,0:T(8,128)} copy(f32[3,6,32,128]{3,2,1,0:T(8,128)S(1)} %copy-done.1) | data formatting | bytes 589824
Async XLA Ops:
  44.0 1.8 %copy-start = (f32[6,6,32,128]{3,2,1,0:T(8,128)S(1)}, f32[6,6,32,128]{3,2,1,0:T(8,128)}, u32[]{:S(2)}) copy-start(f32[6,6,32,128]{3,2,1,0:T(8,128)} %get-tuple-element.7) | copy-start | bytes 1769476
  45.8 1.1 %copy-start.1 = (f32[3,6,32,128]{3,2,1,0:T(8,128)S(1)}, f32[3,6,32,128]{3,2,1,0:T(8,128)}, u32[]{:S(2)}) copy-start(f32[3,6,32,128]{3,2,1,0:T(8,128)} %get-tuple-element.8) | copy-start | bytes 884740

commit v2 on v1

--- a/solution.py
+++ b/solution.py
@@ -70,6 +70,7 @@
     payload,
     packed,
     first_hop,
+    regrouped,
     second_hop,
     spot_rows,
     spot_cols,
@@ -78,7 +79,6 @@
     y_send,
     y_recv,
     in_sem,
-    out_sem,
     hop_send,
     hop_recv,
     face_send,
@@ -112,18 +112,36 @@
     for load in loads:
         load.start()
 
+    half_x, half_y = n_x // 2, n_y // 2
+    my_a = lax.rem(gx, half_x) * 2 + lax.rem(gy, 2)
+    my_b = (gx // half_x) * half_y + gy // 2
+    size_a, size_b = n_x, n_y
+
+    def at_a(a):
+        return ((gx // half_x) * half_x + a // 2, (gy // 2) * 2 + lax.rem(a, 2))
+
+    def at_b(b):
+        return ((b // half_y) * half_x + lax.rem(gx, half_x), lax.rem(b, half_y) * 2 + lax.rem(gy, 2))
+
+    up_x = (lax.rem(gx + 1, n_x), gy)
+    down_x = (lax.rem(gx + n_x - 1, n_x), gy)
+    up_y = (gx, lax.rem(gy + 1, n_y))
+    down_y = (gx, lax.rem(gy + n_y - 1, n_y))
+    around = (up_x, down_x, up_y, down_y)
+
     barrier = pltpu.get_barrier_semaphore()
 
-    def greet_x(i, _):
-        pl.semaphore_signal(barrier, inc=1, device_id=(lax.rem(gx + i, n_x), gy), device_id_type=MESH)
-        return 0
-
-    def greet_y(i, _):
-        pl.semaphore_signal(barrier, inc=1, device_id=(gx, lax.rem(gy + i, n_y)), device_id_type=MESH)
-        return 0
-
-    lax.fori_loop(1, n_x, greet_x, 0)
-    lax.fori_loop(1, n_y, greet_y, 0)
+    def greet(place, me, size):
+        def run(i, _):
+            pl.semaphore_signal(barrier, inc=1, device_id=place(lax.rem(me + i, size)), device_id_type=MESH)
+            return 0
+
+        lax.fori_loop(1, size, run, 0)
+
+    greet(at_a, my_a, size_a)
+    greet(at_b, my_b, size_b)
+    for target in around:
+        pl.semaphore_signal(barrier, inc=1, device_id=target, device_id_type=MESH)
 
     blank = jnp.zeros((ZPAD, width, LANES), jnp.float32)
     for ref, comps in ((speed, SPEED_ALL), (tension, (SXZ, SYZ, SZZ))):
@@ -149,19 +167,21 @@
     payload[pl.ds(samples, 1), :] = (cells // LANES).astype(jnp.float32)
     payload[pl.ds(samples + 1, 1), :] = (cells % LANES).astype(jnp.float32)
     load_all = payload[...]
-    parts = [jnp.where(slot == float(s), load_all, 0.0) for s in range(CAP)]
-    parts.append(jnp.zeros((LANES - CAP * FEATURES, rows), jnp.float32))
-    bundle = jnp.concatenate(parts, axis=0)
-    outgoing = sum(dot_nt(named_16, piece) for piece in pieces(bundle))
-    packed[...] = outgoing.reshape(n_x, n_y, 1, LANES)
+    at_x, at_y = names // n_y, lax.rem(names, n_y)
+    to_a = lax.rem(at_x, half_x) * 2 + lax.rem(at_y, 2)
+    to_b = (at_x // half_x) * half_y + at_y // 2
+    row_to = to_a * (size_b // CAP) + to_b // CAP
+    group = lax.rem(to_b, CAP).astype(jnp.float32) * CAP + slot
+    spread = [jnp.where((group == float(g)) & (slot < CAP), load_all, 0.0) for g in range(CAP * CAP)]
+    bundle = jnp.concatenate(spread, axis=0)
+    lines = size_a * size_b // CAP
+    aimed = (lax.broadcasted_iota(jnp.int32, (lines, rows), 0) == row_to).astype(jnp.float32).astype(jnp.bfloat16)
+    outgoing = sum(dot_nt(aimed, piece) for piece in pieces(bundle))
+    packed[...] = outgoing.reshape(size_a, size_b // CAP, 1, LANES)
 
     lane = lax.broadcasted_iota(jnp.int32, (width, LANES), 1)
 
     def face_copies(phase):
-        up_x = (lax.rem(gx + 1, n_x), gy)
-        down_x = (lax.rem(gx + n_x - 1, n_x), gy)
-        up_y = (gx, lax.rem(gy + 1, n_y))
-        down_y = (gx, lax.rem(gy + n_y - 1, n_y))
         return [
             pltpu.make_async_remote_copy(
                 src_ref=send.at[phase, side],
@@ -286,7 +306,10 @@
             for k, rate in enumerate((rate_x, rate_y, rate_z)):
                 if phase > 0:
                     rate = rate + source[3 * (phase // 2) + k, z]
-                speed[k, z + ZPAD, inner, :] = speed[k, z + ZPAD, inner, :] + factor * rate
+                value = speed[k, z + ZPAD, inner, :] + factor * rate
+                speed[k, z + ZPAD, inner, :] = value
+                if phase == EXCHANGES - 2:
+                    vel_out[k, z] = value
             return 0
 
         lax.fori_loop(0, depth, plane, 0, unroll=True)
@@ -319,43 +342,47 @@
                 (SXZ, stiff * gxz),
                 (SYZ, stiff * gyz),
             ):
-                tension[comp, z + ZPAD, inner, :] = tension[comp, z + ZPAD, inner, :] + change
+                value = tension[comp, z + ZPAD, inner, :] + change
+                if last:
+                    str_out[comp, z] = value
+                else:
+                    tension[comp, z + ZPAD, inner, :] = value
             if last:
                 f = [strain[comp, z].astype(jnp.float32) for comp in range(6)]
                 a = [accel[comp, z].astype(jnp.float32) for comp in range(3)]
                 v = [speed[comp, z + ZPAD, inner, :] for comp in range(3)]
-                kern[0, z] = kern[0, z] - STEP_DT * (f[SXX] + f[SYY] + f[SZZ]) * spread
-                kern[1, z] = kern[1, z] - 2.0 * STEP_DT * (
+                kern_out[0, z] = kern[0, z] - STEP_DT * (f[SXX] + f[SYY] + f[SZZ]) * spread
+                kern_out[1, z] = kern[1, z] - 2.0 * STEP_DT * (
                     f[SXX] * exx + f[SYY] * eyy + f[SZZ] * ezz + f[SXY] * gxy + f[SXZ] * gxz + f[SYZ] * gyz
                 )
-                kern[2, z] = kern[2, z] - STEP_DT * (a[0] * v[0] + a[1] * v[1] + a[2] * v[2])
+                kern_out[2, z] = kern[2, z] - STEP_DT * (a[0] * v[0] + a[1] * v[1] + a[2] * v[2])
             return 0
 
         lax.fori_loop(0, depth, plane, 0, unroll=True)
 
     loads[3].wait()
     pack_faces(0, tension, STRESS_X, STRESS_Y)
-    pl.semaphore_wait(barrier, n_x + n_y - 2)
-
-    def hop_x(i):
-        to = lax.rem(gx + i, n_x)
+    pl.semaphore_wait(barrier, size_a + size_b - 2 + len(around))
+
+    def hop_a(i):
+        to = lax.rem(my_a + i, size_a)
         return pltpu.make_async_remote_copy(
             src_ref=packed.at[to],
-            dst_ref=first_hop.at[:, gx],
+            dst_ref=first_hop.at[lax.rem(my_a, CAP), :, my_a // CAP],
             send_sem=hop_send.at[0, i],
             recv_sem=hop_recv.at[0, i],
-            device_id=(to, gy),
+            device_id=at_a(to),
             device_id_type=MESH,
         )
 
-    def hop_y(i):
-        to = lax.rem(gy + i, n_y)
+    def hop_b(i):
+        to = lax.rem(my_b + i, size_b)
         return pltpu.make_async_remote_copy(
-            src_ref=first_hop.at[to],
-            dst_ref=second_hop.at[gy],
+            src_ref=regrouped.at[to // CAP, lax.rem(to, CAP)],
+            dst_ref=second_hop.at[my_b],
             send_sem=hop_send.at[1, i],
             recv_sem=hop_recv.at[1, i],
-            device_id=(gx, to),
+            device_id=at_b(to),
             device_id_type=MESH,
         )
 
@@ -380,35 +407,48 @@
 
         return run
 
-    own_x = pltpu.make_async_copy(packed.at[gx], first_hop.at[:, gx], hop_recv.at[0, 0])
-    own_y = pltpu.make_async_copy(first_hop.at[gy], second_hop.at[gy], hop_recv.at[1, 0])
-    lax.fori_loop(1, n_x, start(hop_x), 0)
-    own_x.start()
+    lax.fori_loop(1, size_a, start(hop_a), 0)
+    own_a = pltpu.make_async_copy(
+        packed.at[my_a], first_hop.at[lax.rem(my_a, CAP), :, my_a // CAP], hop_recv.at[0, 0]
+    )
+    own_a.start()
     for copy in face_copies(0):
         copy.start()
-    own_x.wait()
-    lax.fori_loop(1, n_x, landed(hop_x), 0)
-    lax.fori_loop(1, n_y, start(hop_y), 0)
-    own_y.start()
+    own_a.wait()
+    lax.fori_loop(1, size_a, landed(hop_a), 0)
+    heaps = [first_hop[p].reshape(lines // CAP, LANES) for p in range(CAP)]
+    span = CAP * FEATURES
+    lane_hop = lax.broadcasted_iota(jnp.int32, (lines // CAP, LANES), 1)
+    for low in range(CAP):
+        merged = None
+        for p in range(CAP):
+            shift = (span * (p - low)) % LANES
+            turned = heaps[p] if shift == 0 else pltpu.roll(heaps[p], shift, 1)
+            merged = turned if p == 0 else jnp.where(lane_hop >= span * p, turned, merged)
+        regrouped[:, low] = merged.reshape(size_b // CAP, size_a // CAP, 1, LANES)
+    lax.fori_loop(1, size_b, start(hop_b), 0)
+    own_b = pltpu.make_async_copy(
+        regrouped.at[my_b // CAP, lax.rem(my_b, CAP)], second_hop.at[my_b], hop_recv.at[1, 0]
+    )
+    own_b.start()
 
     take_faces(0, tension, STRESS_X)
     loads[4].wait()
     loads[5].wait()
     push_speed(0)
 
-    own_y.wait()
-    lax.fori_loop(1, n_y, landed(hop_y), 0)
-    arrived = second_hop[...].reshape(tiles, LANES).T
-    row_of = lax.broadcasted_iota(jnp.int32, (depth * width, tiles), 0).astype(jnp.float32)
-    col_of = lax.broadcasted_iota(jnp.int32, (LANES, tiles), 0).astype(jnp.float32)
-    values = []
-    for s in range(CAP):
-        group = arrived[s * FEATURES : (s + 1) * FEATURES, :]
-        span = pl.ds(s * tiles, tiles)
-        spot_rows[:, span] = (row_of == group[samples : samples + 1]).astype(jnp.float32).astype(jnp.bfloat16)
-        spot_cols[:, span] = (col_of == group[samples + 1 : samples + 2]).astype(jnp.float32).astype(jnp.bfloat16)
-        values.append(group)
-    amounts = pieces(jnp.concatenate(values, axis=1))
+    own_b.wait()
+    lax.fori_loop(1, size_b, landed(hop_b), 0)
+    arrived = second_hop[...].reshape(lines, LANES)
+    arrived = jnp.concatenate([arrived, pltpu.roll(arrived, LANES // 2, 1)], axis=0).T
+    heap = LANES // 2 // FEATURES
+    values = jnp.concatenate([arrived[g * FEATURES : (g + 1) * FEATURES] for g in range(heap)], axis=1)
+    entries = CAP * tiles
+    row_of = lax.broadcasted_iota(jnp.int32, (depth * width, entries), 0).astype(jnp.float32)
+    col_of = lax.broadcasted_iota(jnp.int32, (LANES, entries), 0).astype(jnp.float32)
+    spot_rows[...] = (row_of == values[samples : samples + 1]).astype(jnp.float32).astype(jnp.bfloat16)
+    spot_cols[...] = (col_of == values[samples + 1 : samples + 2]).astype(jnp.float32).astype(jnp.bfloat16)
+    amounts = pieces(values)
 
     def lay_sources(step):
         columns = spot_cols[...]
@@ -431,8 +471,6 @@
             loads[6].wait()
             loads[7].wait()
         else:
-            out_speed = pltpu.make_async_copy(speed.at[:, planes, inner, :], vel_out, out_sem.at[0])
-            out_speed.start()
             for load in loads[8:]:
                 load.wait()
         take_faces(phase, speed, SPEED_ALL)
@@ -444,19 +482,19 @@
                 copy.start()
             take_faces(phase, tension, STRESS_X)
             push_speed(phase)
-    out_rest = [
-        pltpu.make_async_copy(tension.at[:, planes, inner, :], str_out, out_sem.at[1]),
-        pltpu.make_async_copy(kern, kern_out, out_sem.at[2]),
-    ]
-    for copy in out_rest:
-        copy.start()
-    lax.fori_loop(1, n_x, sent(hop_x), 0)
-    lax.fori_loop(1, n_y, sent(hop_y), 0)
+    lax.fori_loop(1, size_a, sent(hop_a), 0)
+    lax.fori_loop(1, size_b, sent(hop_b), 0)
     for phase in range(EXCHANGES):
         for copy in face_copies(phase):
             copy.wait_send()
-    out_speed.wait()
-    for copy in out_rest:
+
+
+def deliver(*refs):
+    sources, targets, sems = refs[:3], refs[3:6], refs[6]
+    copies = [pltpu.make_async_copy(src, dst, sems.at[i]) for i, (src, dst) in enumerate(zip(sources, targets))]
+    for copy in copies:
+        copy.start()
+    for copy in copies:
         copy.wait()
 
 
@@ -482,15 +520,15 @@
     padded = (depth + 2 * ZPAD, width + 2 * MARGIN, lanes)
     f32, b16 = jnp.float32, jnp.bfloat16
     far = pl.BlockSpec(memory_space=pltpu.HBM)
-    return pl.pallas_call(
+    results = pl.pallas_call(
         functools.partial(kernel, n_x, n_y),
         out_shape=[
-            jax.ShapeDtypeStruct(velocity.shape, f32),
-            jax.ShapeDtypeStruct(stress.shape, f32),
-            jax.ShapeDtypeStruct(kernels.shape, f32),
+            pltpu.VMEM(velocity.shape, f32),
+            pltpu.VMEM(stress.shape, f32),
+            pltpu.VMEM(kernels.shape, f32),
         ],
         in_specs=[far] * 11 + [pl.BlockSpec(memory_space=pltpu.SMEM)],
-        out_specs=[far] * 3,
+        out_specs=[pl.BlockSpec(memory_space=pltpu.VMEM)] * 3,
         scratch_shapes=[
             pltpu.VMEM((3, *padded), f32),
             pltpu.VMEM((6, *padded), f32),
@@ -505,9 +543,10 @@
             pltpu.VMEM((1, rows), jnp.int32),
             pltpu.VMEM((3 * STEPS, *buoyancy.shape), f32),
             pltpu.VMEM((FEATURES, rows), f32),
-            pltpu.VMEM((n_x, n_y, 1, lanes), f32),
-            pltpu.VMEM((n_y, n_x, 1, lanes), f32),
-            pltpu.VMEM((n_y, n_x, 1, lanes), f32),
+            pltpu.VMEM((n_x, n_y // CAP, 1, lanes), f32),
+            pltpu.VMEM((CAP, n_y // CAP, n_x // CAP, 1, lanes), f32),
+            pltpu.VMEM((n_y // CAP, CAP, n_x // CAP, 1, lanes), f32),
+            pltpu.VMEM((n_y, n_x // CAP, 1, lanes), f32),
             pltpu.VMEM((depth * width, CAP * tiles), b16),
             pltpu.VMEM((lanes, CAP * tiles), b16),
             pltpu.VMEM((EXCHANGES, 2, strips, 2, lanes), f32),
@@ -515,29 +554,40 @@
             pltpu.VMEM((EXCHANGES, 2, width, lanes), f32),
             pltpu.VMEM((EXCHANGES, 2, width, lanes), f32),
             pltpu.SemaphoreType.DMA((11,)),
-            pltpu.SemaphoreType.DMA((3,)),
             pltpu.SemaphoreType.DMA((2, max(n_x, n_y))),
             pltpu.SemaphoreType.DMA((2, max(n_x, n_y))),
             pltpu.SemaphoreType.DMA((EXCHANGES, 4)),
             pltpu.SemaphoreType.DMA((EXCHANGES, 4)),
         ],
         compiler_params=pltpu.CompilerParams(
-            collective_id=0, has_side_effects=True, vmem_limit_bytes=60 * 1024 * 1024
+            collective_id=0, has_side_effects=True, vmem_limit_bytes=48 * 1024 * 1024
         ),
     )(
-        velocity,
-        stress,
-        lame_first,
-        shear,
-        buoyancy,
-        fwd_strain,
-        fwd_accel,
-        kernels,
-        station_trace.T,
-        station_tile.reshape(1, rows),
-        station_cell.reshape(1, rows),
+        *(
+            pltpu.with_memory_space_constraint(array, pltpu.HBM)
+            for array in (
+                velocity,
+                stress,
+                lame_first,
+                shear,
+                buoyancy,
+                fwd_strain,
+                fwd_accel,
+                kernels,
+                station_trace.T,
+                station_tile.reshape(1, rows),
+                station_cell.reshape(1, rows),
+            )
+        ),
         station_count,
     )
+    return pl.pallas_call(
+        deliver,
+        out_shape=[pltpu.HBM(array.shape, f32) for array in (velocity, stress, kernels)],
+        in_specs=[pl.BlockSpec(memory_space=pltpu.VMEM)] * 3,
+        out_specs=[far] * 3,
+        scratch_shapes=[pltpu.SemaphoreType.DMA((3,))],
+    )(*(pltpu.with_memory_space_constraint(array, pltpu.VMEM) for array in results))
 
 
 def solution(mesh):

time: 48.1 us -> 40.8 us (0.85)
  local copies, waits for them, and re-layouts: 3.6 us -> 0 us
  Pallas kernels: 42.7 us -> 39.3 us
    unnamed x7 -> x0, local copies, waits for them, and re-layouts: 3.6 us -> none
    pallas_call x1 -> x2, Pallas kernels: 42.7 us -> 39.3 us  [the longest x1 38.3 us: body(): pl.pallas_call(functools.partial(kernel, n_x, n_y), out_shape=[pltpu.VMEM...]
where the time goes in v2:
time: 40.8 us; the launch traced here: 40.6 us
  Pallas kernels  39.3 us (96%)
  between operations  1.29 us (3%)
    pallas_call x1, Pallas kernels, body(): pl.pallas_call(functools.partial(kernel, n_x, n_y), out_shape=[pltpu.VMEM...  38.3 us
    pallas_call x1, Pallas kernels, body(): pl.pallas_call(deliver, out_shape=[pltpu.HBM(array.shape, f32) for array...  1.03 us

profile of v2, /device:TPU:1, one launch (start us, length us, event | category | flops | bytes accessed | tf_op | source)
XLA Modules:
  0.0 40.6 jit_solution(6989240831494706373)
XLA Ops:
  1.3 38.3 %shard_map.139 = (f32[3,6,32,128]{3,2,1,0:T(8,128)S(1)}, f32[6,6,32,128]{3,2,1,0:T(8,128)S(1)}, f32[3,6,32,128]{3,2,1,0:T(8,128)S(1)}) custom-call(f32[3,6,32,128]{3,2,1,0:T(8,128)} %vel_in.1, f32[6,6,32,128]{3,2,1,0:T(8,128)} %str_in.1, f32[6,32,128]{2,1,0:T(8,128)} %lame_in.1, f32[6,32,128]{2,1,0:T(8,128)} %shear_in.1, f32[6,32,128]{2,1,0:T(8,128)} %buoy_in.1, ...), custom_call_target="tpu_custom_call" | custom-call | tf_op jit(solution)/shard_map/pallas_call | solution.py:523
  39.6 1.0 %shard_map.140 = (f32[3,6,32,128]{3,2,1,0:T(8,128)}, f32[6,6,32,128]{3,2,1,0:T(8,128)}, f32[3,6,32,128]{3,2,1,0:T(8,128)}) custom-call(f32[3,6,32,128]{3,2,1,0:T(8,128)S(1)} %get-tuple-element.6.refs_0_, f32[6,6,32,128]{3,2,1,0:T(8,128)S(1)} %get-tuple-element.7.refs_1_, f32[3,6,32,128]{3,2,1,0:T(8,128)S(1)} %get-tuple-element.8.refs_2_), custom_call_target="tpu_custom_call" | custom-call | tf_op jit(solution)/shard_map/pallas_call | solution.py:584

commit v3 on v2

v3 whole, which is shorter than its diff:
```python
import functools

import jax
import jax.numpy as jnp
from jax import lax
from jax.experimental import pallas as pl
from jax.experimental.pallas import tpu as pltpu
from jax.sharding import PartitionSpec as P

STEPS = 2
CAP = 4
C_NEAR = 9.0 / 8.0
C_FAR = -1.0 / 24.0
STEP_DT = 0.25
MESH = pl.DeviceIdType.MESH

LANES = 128
FEATURES = 8
MARGIN = 8
ZPAD = 2
SXX, SXZ, SXY, SYY, SYZ, SZZ = range(6)
LAME, SHEAR, BUOY = range(3)
STRIP = 10
KEPT = 4
REACH = STRIP - KEPT
WINGS = LANES // 2 - 4


def pieces(value):
    high = value.astype(jnp.bfloat16)
    rest = value - high.astype(jnp.float32)
    middle = rest.astype(jnp.bfloat16)
    low = (rest - middle.astype(jnp.float32)).astype(jnp.bfloat16)
    return high, middle, low


def dot_nt(left, right):
    return lax.dot_general(left, right, (((1,), (1,)), ((), ())), preferred_element_type=jnp.float32)


def kernel(
    n_x,
    n_y,
    vel_in,
    str_in,
    lame_in,
    shear_in,
    buoy_in,
    strain_in,
    accel_in,
    kern_in,
    trace_in,
    tile_in,
    cell_in,
    count,
    vel_out,
    str_out,
    kern_out,
    speed,
    tension,
    solid,
    strain,
    accel,
    kern,
    trace,
    tile,
    cell,
    source,
    payload,
    packed,
    first_hop,
    regrouped,
    second_hop,
    spot_rows,
    spot_cols,
    speed_wing,
    tension_wing,
    solid_wing,
    source_wing,
    *rest,
):
    x_send, x_recv, wing_send, wing_recv, corner_recv = (rest[3 * i : 3 * i + 3] for i in range(5))
    in_sem, hop_send, hop_recv, face_send, face_recv = rest[15:]
    depth, width = buoy_in.shape[0], buoy_in.shape[1]
    rows = trace.shape[1]
    tiles = n_x * n_y
    gx, gy = lax.axis_index("gx"), lax.axis_index("gy")
    inner = pl.ds(MARGIN, width)
    planes = pl.ds(ZPAD, depth)

    loads = [
        pltpu.make_async_copy(src, dst, in_sem.at[i])
        for i, (src, dst) in enumerate(
            (
                (trace_in, trace),
                (tile_in, tile),
                (cell_in, cell),
                (str_in, tension.at[:, planes, inner, :]),
                (vel_in, speed.at[:, planes, inner, :]),
                (buoy_in, solid.at[BUOY, :, inner, :]),
                (lame_in, solid.at[LAME, :, inner, :]),
                (shear_in, solid.at[SHEAR, :, inner, :]),
                (strain_in, strain),
                (accel_in, accel),
                (kern_in, kern),
            )
        )
    ]
    for load in loads:
        load.start()

    half_x, half_y = n_x // 2, n_y // 2
    my_a = lax.rem(gx, half_x) * 2 + lax.rem(gy, 2)
    my_b = (gx // half_x) * half_y + gy // 2
    size_a, size_b = n_x, n_y

    def at_a(a):
        return ((gx // half_x) * half_x + a // 2, (gy // 2) * 2 + lax.rem(a, 2))

    def at_b(b):
        return ((b // half_y) * half_x + lax.rem(gx, half_x), lax.rem(b, half_y) * 2 + lax.rem(gy, 2))

    up_x = (lax.rem(gx + 1, n_x), gy)
    down_x = (lax.rem(gx + n_x - 1, n_x), gy)
    up_y = (gx, lax.rem(gy + 1, n_y))
    down_y = (gx, lax.rem(gy + n_y - 1, n_y))
    corners = tuple((x, y) for x in (down_x[0], up_x[0]) for y in (down_y[1], up_y[1]))
    around = (down_x, up_x, down_y, up_y) + corners

    barrier = pltpu.get_barrier_semaphore()

    def greet(place, me, size):
        def run(i, _):
            pl.semaphore_signal(barrier, inc=1, device_id=place(lax.rem(me + i, size)), device_id_type=MESH)
            return 0

        lax.fori_loop(1, size, run, 0)

    greet(at_a, my_a, size_a)
    greet(at_b, my_b, size_b)
    for target in around:
        pl.semaphore_signal(barrier, inc=1, device_id=target, device_id_type=MESH)

    blank = jnp.zeros((ZPAD, width + 2 * MARGIN, LANES), jnp.float32)
    for ref, comps in ((speed, (0, 1, 2)), (tension, (SXZ, SYZ, SZZ))):
        for comp in comps:
            ref[comp, pl.ds(0, ZPAD)] = blank
            ref[comp, pl.ds(ZPAD + depth, ZPAD)] = blank

    for load in loads[:3]:
        load.wait()
    names = tile[...]
    line = lax.broadcasted_iota(jnp.int32, (tiles, rows), 0)
    named = (line == names).astype(jnp.float32)
    named_16 = named.astype(jnp.bfloat16)
    earlier = (
        lax.broadcasted_iota(jnp.int32, (rows, rows), 0) < lax.broadcasted_iota(jnp.int32, (rows, rows), 1)
    ).astype(jnp.float32).astype(jnp.bfloat16)
    ahead = jnp.dot(named_16, earlier, preferred_element_type=jnp.float32)
    slot = jnp.sum(named * ahead, axis=0, keepdims=True)
    live = lax.broadcasted_iota(jnp.int32, (1, rows), 1) < count[0]
    cells = cell[...]
    samples = trace.shape[0]
    payload[pl.ds(0, samples), :] = jnp.where(live, trace[...], 0.0)
    payload[pl.ds(samples, 1), :] = (cells // LANES).astype(jnp.float32)
    payload[pl.ds(samples + 1, 1), :] = (cells % LANES).astype(jnp.float32)
    load_all = payload[...]
    at_x, at_y = names // n_y, lax.rem(names, n_y)
    to_a = lax.rem(at_x, half_x) * 2 + lax.rem(at_y, 2)
    to_b = (at_x // half_x) * half_y + at_y // 2
    row_to = to_a * (size_b // CAP) + to_b // CAP
    group = lax.rem(to_b, CAP).astype(jnp.float32) * CAP + slot
    spread = [jnp.where((group == float(g)) & (slot < CAP), load_all, 0.0) for g in range(CAP * CAP)]
    bundle = jnp.concatenate(spread, axis=0)
    lines = size_a * size_b // CAP
    aimed = (lax.broadcasted_iota(jnp.int32, (lines, rows), 0) == row_to).astype(jnp.float32).astype(jnp.bfloat16)
    outgoing = sum(dot_nt(aimed, piece) for piece in pieces(bundle))
    packed[...] = outgoing.reshape(size_a, size_b // CAP, 1, LANES)

    lane_row = lax.broadcasted_iota(jnp.int32, (1, LANES), 1)
    turn = lax.rem(lane_row, STRIP)
    level = lax.rem(lane_row // STRIP, depth)
    from_up = (lane_row < WINGS) & (turn >= KEPT)
    from_down = (lane_row >= WINGS) & (turn < REACH)
    below = MARGIN + width

    def face_copies(e):
        strips = x_send[e].shape[1]
        count = wing_send[e].shape[0]
        tail = pl.ds(strips - count, count)
        moves = [
            (x_send[e].at[0], x_recv[e].at[0], down_x),
            (x_send[e].at[1], x_recv[e].at[1], up_x),
            (wing_send[e], wing_recv[e].at[0], down_y),
            (wing_send[e], wing_recv[e].at[1], up_y),
        ]
        if e < 2:
            for k, target in enumerate(corners):
                moves.append((x_send[e].at[k // 2, tail], corner_recv[e].at[k // 2, k % 2], target))
        return [
            pltpu.make_async_remote_copy(
                src_ref=src,
                dst_ref=dst,
                send_sem=face_send.at[e, k],
                recv_sem=face_recv.at[e, k],
                device_id=target,
                device_id_type=MESH,
            )
            for k, (src, dst, target) in enumerate(moves)
        ]

    def pack_faces(e, fields):
        reach = x_send[e].shape[2]
        for i, (ref, comp, first) in enumerate(fields):
            def strip(z, heap, i=i, ref=ref, comp=comp, first=first):
                plane = ref[comp, z + first, inner, :]
                x_send[e][0, i * depth + z] = ref[comp, z + first, pl.ds(MARGIN, reach), :]
                x_send[e][1, i * depth + z] = ref[comp, z + first, pl.ds(below - reach, reach), :]
                start = z * STRIP
                low, high = heap
                low = jnp.where(lane_row >= start, pltpu.roll(plane, start + KEPT, 1), low)
                high = jnp.where(lane_row >= WINGS + start, pltpu.roll(plane, WINGS + start + REACH, 1), high)
                return low, high

            empty = jnp.zeros((width, LANES), jnp.float32)
            low, high = lax.fori_loop(0, depth, strip, (empty, empty), unroll=True)
            wing = jnp.where(lane_row >= WINGS, high, low)
            wing_send[e][i] = wing
            if e < 2:
                x_send[e][0, len(fields) * depth + i] = wing[:reach]
                x_send[e][1, len(fields) * depth + i] = wing[width - reach :]
        for copy in face_copies(e):
            copy.start()

    def take_faces(e, fields):
        reach = x_send[e].shape[2]
        for copy in face_copies(e):
            copy.wait_recv()

        def clear(at_edge, *refs):
            @pl.when(at_edge)
            def _():
                for ref in refs:
                    ref[...] = jnp.zeros(ref.shape, jnp.float32)

        corner = corner_recv[e]
        both = e < 2
        clear(gy == n_y - 1, wing_recv[e].at[0], *([corner.at[0, 0], corner.at[1, 0]] if both else []))
        clear(gy == 0, wing_recv[e].at[1], *([corner.at[0, 1], corner.at[1, 1]] if both else []))
        clear(gx == n_x - 1, x_recv[e].at[0], *([corner.at[0]] if both else []))
        clear(gx == 0, x_recv[e].at[1], *([corner.at[1]] if both else []))

        def mixed(up, down, own):
            return jnp.where(from_up, up, jnp.where(from_down, down, own))

        for i, (ref, comp, first, wing, at) in enumerate(fields):
            def rows_of(z, _, i=i, ref=ref, comp=comp, first=first):
                ref[comp, z + first, pl.ds(below, reach), :] = x_recv[e][0, i * depth + z]
                ref[comp, z + first, pl.ds(MARGIN - reach, reach), :] = x_recv[e][1, i * depth + z]
                return 0

            lax.fori_loop(0, depth, rows_of, 0, unroll=True)
            wing[at, inner, :] = mixed(wing_recv[e][0, i], wing_recv[e][1, i], wing_send[e][i])
            if both:
                for side, start in ((0, below), (1, MARGIN - reach)):
                    wing[at, pl.ds(start, reach), :] = mixed(
                        corner[side, 0, i], corner[side, 1, i], x_recv[e][side, len(fields) * depth + i]
                    )

    def difference(at, upward):
        if upward:
            return C_NEAR * (at(1) - at(0)) + C_FAR * (at(2) - at(-1))
        return C_NEAR * (at(0) - at(-1)) + C_FAR * (at(1) - at(-2))

    def tile_part(z, start, count):
        def along_z(ref, comp, upward):
            return difference(lambda o: ref[comp, z + ZPAD + o, pl.ds(start, count), :], upward)

        def along_x(ref, comp, upward):
            return difference(lambda o: ref[comp, z + ZPAD, pl.ds(start + o, count), :], upward)

        def along_y(ref, comp, upward):
            wing = (speed_wing if ref is speed else tension_wing)[comp, pl.ds(start, count), :]
            centre = ref[comp, z + ZPAD, pl.ds(start, count), :]
            side = jnp.where(
                lane_row < LANES // 2,
                pltpu.roll(wing, LANES - KEPT - z * STRIP, 1),
                pltpu.roll(wing, LANES - REACH - WINGS - z * STRIP, 1),
            )

            def at(o):
                if o == 0:
                    return centre
                if o > 0:
                    return pltpu.roll(jnp.where(lane_row < o, side, centre), LANES - o, 1)
                return pltpu.roll(jnp.where(lane_row >= LANES + o, side, centre), -o, 1)

            return difference(at, upward)

        return along_x, along_y, along_z

    def wing_part(start, count):
        def held(ref, comp, o=0):
            return (speed_wing if ref is speed else tension_wing)[comp, pl.ds(start + o, count), :]

        def along_z(ref, comp, upward):
            value = held(ref, comp)

            def at(o):
                if o == 0:
                    return value
                inside = (level + o >= 0) & (level + o < depth)
                return jnp.where(inside, pltpu.roll(value, (-o * STRIP) % LANES, 1), 0.0)

            return difference(at, upward)

        def along_x(ref, comp, upward):
            return difference(lambda o: held(ref, comp, o), upward)

        def along_y(ref, comp, upward):
            value = held(ref, comp)
            return difference(lambda o: value if o == 0 else pltpu.roll(value, -o % LANES, 1), upward)

        return along_x, along_y, along_z

    def rates(along_x, along_y, along_z):
        return (
            along_x(tension, SXX, True) + along_y(tension, SXY, False) + along_z(tension, SXZ, False),
            along_x(tension, SXY, False) + along_y(tension, SYY, True) + along_z(tension, SYZ, False),
            along_x(tension, SXZ, False) + along_y(tension, SYZ, False) + along_z(tension, SZZ, True),
        )

    def strains(along_x, along_y, along_z):
        exx = along_x(speed, 0, False)
        eyy = along_y(speed, 1, False)
        ezz = along_z(speed, 2, False)
        gxy = along_y(speed, 0, True) + along_x(speed, 1, True)
        gxz = along_z(speed, 0, True) + along_x(speed, 2, True)
        gyz = along_z(speed, 1, True) + along_y(speed, 2, True)
        return exx, eyy, ezz, gxy, gxz, gyz

    def changes(strained, lame, shear):
        exx, eyy, ezz, gxy, gxz, gyz = strained
        stiff = STEP_DT * shear
        common = STEP_DT * lame * (exx + eyy + ezz)
        return (
            (SXX, common + 2.0 * stiff * exx),
            (SYY, common + 2.0 * stiff * eyy),
            (SZZ, common + 2.0 * stiff * ezz),
            (SXY, stiff * gxy),
            (SXZ, stiff * gxz),
            (SYZ, stiff * gyz),
        )

    def push_speed(margin, step, final):
        start, count = MARGIN - margin, width + 2 * margin
        rows_at = pl.ds(start, count)

        def plane(z, _):
            factor = STEP_DT * solid[BUOY, z, rows_at, :]
            for k, rate in enumerate(rates(*tile_part(z, start, count))):
                if step > 0:
                    rate = rate + source[3 * step + k, z, rows_at, :]
                value = speed[k, z + ZPAD, rows_at, :] + factor * rate
                speed[k, z + ZPAD, rows_at, :] = value
                if final:
                    vel_out[k, z] = value[margin : margin + width]
            return 0

        lax.fori_loop(0, depth, plane, 0, unroll=True)
        if margin > 0:
            factor = STEP_DT * solid_wing[BUOY, inner, :]
            for k, rate in enumerate(rates(*wing_part(MARGIN, width))):
                change = factor * (rate + source_wing[k, inner, :])
                speed_wing[k, inner, :] = speed_wing[k, inner, :] + change

    def add_source(step):
        def plane(z, _):
            factor = STEP_DT * solid[BUOY, z, inner, :]
            for k in range(3):
                speed[k, z + ZPAD, inner, :] = (
                    speed[k, z + ZPAD, inner, :] + factor * source[3 * step + k, z, inner, :]
                )
            return 0

        lax.fori_loop(0, depth, plane, 0, unroll=True)

    def push_stress(margin, final):
        start, count = MARGIN - margin, width + 2 * margin
        rows_at = pl.ds(start, count)

        def plane(z, _):
            strained = strains(*tile_part(z, start, count))
            for comp, change in changes(strained, solid[LAME, z, rows_at, :], solid[SHEAR, z, rows_at, :]):
                value = tension[comp, z + ZPAD, rows_at, :] + change
                if final:
                    str_out[comp, z] = value
                else:
                    tension[comp, z + ZPAD, rows_at, :] = value
            if final:
                exx, eyy, ezz, gxy, gxz, gyz = strained
                f = [strain[comp, z].astype(jnp.float32) for comp in range(6)]
                a = [accel[comp, z].astype(jnp.float32) for comp in range(3)]
                v = [speed[comp, z + ZPAD, inner, :] for comp in range(3)]
                kern_out[0, z] = kern[0, z] - STEP_DT * (f[SXX] + f[SYY] + f[SZZ]) * (exx + eyy + ezz)
                kern_out[1, z] = kern[1, z] - 2.0 * STEP_DT * (
                    f[SXX] * exx + f[SYY] * eyy + f[SZZ] * ezz + f[SXY] * gxy + f[SXZ] * gxz + f[SYZ] * gyz
                )
                kern_out[2, z] = kern[2, z] - STEP_DT * (a[0] * v[0] + a[1] * v[1] + a[2] * v[2])
            return 0

        lax.fori_loop(0, depth, plane, 0, unroll=True)
        if margin > 0:
            near = margin // 2
            near_at = pl.ds(MARGIN - near, width + 2 * near)
            strained = strains(*wing_part(MARGIN - near, width + 2 * near))
            for comp, change in changes(strained, solid_wing[LAME, near_at, :], solid_wing[SHEAR, near_at, :]):
                tension_wing[comp, near_at, :] = tension_wing[comp, near_at, :] + change

    pl.semaphore_wait(barrier, size_a + size_b - 2 + len(around))

    def hop_a(i):
        to = lax.rem(my_a + i, size_a)
        return pltpu.make_async_remote_copy(
            src_ref=packed.at[to],
            dst_ref=first_hop.at[lax.rem(my_a, CAP), :, my_a // CAP],
            send_sem=hop_send.at[0, i],
            recv_sem=hop_recv.at[0, i],
            device_id=at_a(to),
            device_id_type=MESH,
        )

    def hop_b(i):
        to = lax.rem(my_b + i, size_b)
        return pltpu.make_async_remote_copy(
            src_ref=regrouped.at[to // CAP, lax.rem(to, CAP)],
            dst_ref=second_hop.at[my_b],
            send_sem=hop_send.at[1, i],
            recv_sem=hop_recv.at[1, i],
            device_id=at_b(to),
            device_id_type=MESH,
        )

    def start(make):
        def run(i, _):
            make(i).start()
            return 0

        return run

    def landed(make):
        def run(i, _):
            make(i).wait_recv()
            return 0

        return run

    def sent(make):
        def run(i, _):
            make(i).wait_send()
            return 0

        return run

    lax.fori_loop(1, size_a, start(hop_a), 0)
    own_a = pltpu.make_async_copy(
        packed.at[my_a], first_hop.at[lax.rem(my_a, CAP), :, my_a // CAP], hop_recv.at[0, 0]
    )
    own_a.start()
    start_fields = [(tension, comp, ZPAD, tension_wing, comp) for comp in range(6)]
    start_fields += [(solid, comp, 0, solid_wing, comp) for comp in range(3)]
    speed_fields = [(speed, comp, ZPAD, speed_wing, comp) for comp in range(3)]
    late_fields = [(source, 3 + comp, 0, source_wing, comp) for comp in range(3)]
    for load in (loads[3], *loads[5:8]):
        load.wait()
    pack_faces(0, [field[:3] for field in start_fields])
    own_a.wait()
    lax.fori_loop(1, size_a, landed(hop_a), 0)
    heaps = [first_hop[p].reshape(lines // CAP, LANES) for p in range(CAP)]
    span = CAP * FEATURES
    lane_hop = lax.broadcasted_iota(jnp.int32, (lines // CAP, LANES), 1)
    for low in range(CAP):
        merged = None
        for p in range(CAP):
            shift = (span * (p - low)) % LANES
            turned = heaps[p] if shift == 0 else pltpu.roll(heaps[p], shift, 1)
            merged = turned if p == 0 else jnp.where(lane_hop >= span * p, turned, merged)
        regrouped[:, low] = merged.reshape(size_b // CAP, size_a // CAP, 1, LANES)
    lax.fori_loop(1, size_b, start(hop_b), 0)
    own_b = pltpu.make_async_copy(
        regrouped.at[my_b // CAP, lax.rem(my_b, CAP)], second_hop.at[my_b], hop_recv.at[1, 0]
    )
    own_b.start()

    take_faces(0, start_fields)
    loads[4].wait()
    push_speed(0, 0, False)

    own_b.wait()
    lax.fori_loop(1, size_b, landed(hop_b), 0)
    arrived = second_hop[...].reshape(lines, LANES)
    arrived = jnp.concatenate([arrived, pltpu.roll(arrived, LANES // 2, 1)], axis=0).T
    heap = LANES // 2 // FEATURES
    values = jnp.concatenate([arrived[g * FEATURES : (g + 1) * FEATURES] for g in range(heap)], axis=1)
    entries = CAP * tiles
    row_of = lax.broadcasted_iota(jnp.int32, (depth * width, entries), 0).astype(jnp.float32)
    col_of = lax.broadcasted_iota(jnp.int32, (LANES, entries), 0).astype(jnp.float32)
    spot_rows[...] = (row_of == values[samples : samples + 1]).astype(jnp.float32).astype(jnp.bfloat16)
    spot_cols[...] = (col_of == values[samples + 1 : samples + 2]).astype(jnp.float32).astype(jnp.bfloat16)
    amounts = pieces(values)

    def lay_sources(step):
        columns = spot_cols[...]
        total = jnp.zeros((depth * width, 3 * LANES), jnp.float32)
        for amount in amounts:
            spread = [columns * amount[3 * step + k : 3 * step + k + 1, :] for k in range(3)]
            total = total + dot_nt(spot_rows[...], jnp.concatenate(spread, axis=0))
        for k in range(3):
            source[3 * step + k, :, inner, :] = total[:, k * LANES : (k + 1) * LANES].reshape(depth, width, LANES)

    lay_sources(0)
    add_source(0)
    pack_faces(1, [field[:3] for field in speed_fields])
    lay_sources(1)
    pack_faces(2, [field[:3] for field in late_fields])
    for load in loads[8:]:
        load.wait()
    take_faces(1, speed_fields)
    push_stress(4, False)
    take_faces(2, late_fields)
    push_speed(2, 1, True)
    push_stress(0, True)
    lax.fori_loop(1, size_a, sent(hop_a), 0)
    lax.fori_loop(1, size_b, sent(hop_b), 0)
    for e in range(3):
        for copy in face_copies(e):
            copy.wait_send()


def deliver(*refs):
    sources, targets, sems = refs[:3], refs[3:6], refs[6]
    copies = [pltpu.make_async_copy(src, dst, sems.at[i]) for i, (src, dst) in enumerate(zip(sources, targets))]
    for copy in copies:
        copy.start()
    for copy in copies:
        copy.wait()


def body(
    velocity,
    stress,
    lame_first,
    shear,
    buoyancy,
    fwd_strain,
    fwd_accel,
    kernels,
    station_trace,
    station_tile,
    station_cell,
    station_count,
):
    n_x, n_y = lax.axis_size("gx"), lax.axis_size("gy")
    depth, width, lanes = buoyancy.shape
    rows = station_trace.shape[0]
    tiles = n_x * n_y
    exchanges = ((9, 4, 1), (3, 6, 1), (3, 2, 0))
    padded = (depth + 2 * ZPAD, width + 2 * MARGIN, lanes)
    f32, b16 = jnp.float32, jnp.bfloat16
    far = pl.BlockSpec(memory_space=pltpu.HBM)
    results = pl.pallas_call(
        functools.partial(kernel, n_x, n_y),
        out_shape=[
            pltpu.VMEM(velocity.shape, f32),
            pltpu.VMEM(stress.shape, f32),
            pltpu.VMEM(kernels.shape, f32),
        ],
        in_specs=[far] * 11 + [pl.BlockSpec(memory_space=pltpu.SMEM)],
        out_specs=[pl.BlockSpec(memory_space=pltpu.VMEM)] * 3,
        scratch_shapes=[
            pltpu.VMEM((3, *padded), f32),
            pltpu.VMEM((6, *padded), f32),
            pltpu.VMEM((3, depth, *padded[1:]), f32),
            pltpu.VMEM(fwd_strain.shape, b16),
            pltpu.VMEM(fwd_accel.shape, b16),
            pltpu.VMEM(kernels.shape, f32),
            pltpu.VMEM(station_trace.shape[::-1], f32),
            pltpu.VMEM((1, rows), jnp.int32),
            pltpu.VMEM((1, rows), jnp.int32),
            pltpu.VMEM((3 * STEPS, depth, *padded[1:]), f32),
            pltpu.VMEM((FEATURES, rows), f32),
            pltpu.VMEM((n_x, n_y // CAP, 1, lanes), f32),
            pltpu.VMEM((CAP, n_y // CAP, n_x // CAP, 1, lanes), f32),
            pltpu.VMEM((n_y // CAP, CAP, n_x // CAP, 1, lanes), f32),
            pltpu.VMEM((n_y, n_x // CAP, 1, lanes), f32),
            pltpu.VMEM((depth * width, CAP * tiles), b16),
            pltpu.VMEM((lanes, CAP * tiles), b16),
            *[pltpu.VMEM((fields, *padded[1:]), f32) for fields in (3, 6, 3, 3)],
            *[pltpu.VMEM((2, fields * (depth + wings), reach, lanes), f32) for fields, reach, wings in exchanges],
            *[pltpu.VMEM((2, fields * (depth + wings), reach, lanes), f32) for fields, reach, wings in exchanges],
            *[pltpu.VMEM((fields, width, lanes), f32) for fields, reach, wings in exchanges],
            *[pltpu.VMEM((2, fields, width, lanes), f32) for fields, reach, wings in exchanges],
            *[pltpu.VMEM((2, 2, fields, reach, lanes), f32) for fields, reach, wings in exchanges],
            pltpu.SemaphoreType.DMA((11,)),
            pltpu.SemaphoreType.DMA((2, max(n_x, n_y))),
            pltpu.SemaphoreType.DMA((2, max(n_x, n_y))),
            pltpu.SemaphoreType.DMA((len(exchanges), 8)),
            pltpu.SemaphoreType.DMA((len(exchanges), 8)),
        ],
        compiler_params=pltpu.CompilerParams(
            collective_id=0, has_side_effects=True, vmem_limit_bytes=48 * 1024 * 1024
        ),
    )(
        *(
            pltpu.with_memory_space_constraint(array, pltpu.HBM)
            for array in (
                velocity,
                stress,
                lame_first,
                shear,
                buoyancy,
                fwd_strain,
                fwd_accel,
                kernels,
                station_trace.T,
                station_tile.reshape(1, rows),
                station_cell.reshape(1, rows),
            )
        ),
        station_count,
    )
    return pl.pallas_call(
        deliver,
        out_shape=[pltpu.HBM(array.shape, f32) for array in (velocity, stress, kernels)],
        in_specs=[pl.BlockSpec(memory_space=pltpu.VMEM)] * 3,
        out_specs=[far] * 3,
        scratch_shapes=[pltpu.SemaphoreType.DMA((3,))],
    )(*(pltpu.with_memory_space_constraint(array, pltpu.VMEM) for array in results))


def solution(mesh):
    tiled = P(None, None, "gx", "gy")
    plane = P(None, "gx", "gy")
    listed = ("gx", "gy")
    return jax.shard_map(
        body,
        mesh=mesh,
        in_specs=(
            tiled,
            tiled,
            plane,
            plane,
            plane,
            tiled,
            tiled,
            tiled,
            P(listed, None),
            P(listed, None),
            P(listed),
            P(listed),
        ),
        out_specs=(tiled, tiled, tiled),
        check_vma=False,
    )
```

time: 40.8 us -> 38.1 us (0.934)
  Pallas kernels: 39.3 us -> 36.7 us
    pallas_call x1, Pallas kernels: 38.3 us -> 35.7 us  [body(): pl.pallas_call(functools.partial(kernel, n_x, n_y), out_shape=[pltpu.VMEM...]
where the time goes in v3:
time: 38.1 us; the launch traced here: 38 us
  Pallas kernels  36.7 us (96%)
  between operations  1.29 us (3%)
    pallas_call x1, Pallas kernels, body(): pl.pallas_call(functools.partial(kernel, n_x, n_y), out_shape=[pltpu.VMEM...  35.7 us
    pallas_call x1, Pallas kernels, body(): pl.pallas_call(deliver, out_shape=[pltpu.HBM(array.shape, f32) for array...  1.03 us

profile of v3, /device:TPU:1, one launch (start us, length us, event | category | flops | bytes accessed | tf_op | source)
XLA Modules:
  0.0 38.0 jit_solution(7292868711416259937)
XLA Ops:
  1.3 35.7 %shard_map.139 = (f32[3,6,32,128]{3,2,1,0:T(8,128)S(1)}, f32[6,6,32,128]{3,2,1,0:T(8,128)S(1)}, f32[3,6,32,128]{3,2,1,0:T(8,128)S(1)}) custom-call(f32[3,6,32,128]{3,2,1,0:T(8,128)} %vel_in.1, f32[6,6,32,128]{3,2,1,0:T(8,128)} %str_in.1, f32[6,32,128]{2,1,0:T(8,128)} %lame_in.1, f32[6,32,128]{2,1,0:T(8,128)} %shear_in.1, f32[6,32,128]{2,1,0:T(8,128)} %buoy_in.1, ...), custom_call_target="tpu_custom_call" | custom-call | tf_op jit(solution)/shard_map/pallas_call | solution.py:571
  36.9 1.0 %shard_map.140 = (f32[3,6,32,128]{3,2,1,0:T(8,128)}, f32[6,6,32,128]{3,2,1,0:T(8,128)}, f32[3,6,32,128]{3,2,1,0:T(8,128)}) custom-call(f32[3,6,32,128]{3,2,1,0:T(8,128)S(1)} %get-tuple-element.6.refs_0_, f32[6,6,32,128]{3,2,1,0:T(8,128)S(1)} %get-tuple-element.7.refs_1_, f32[3,6,32,128]{3,2,1,0:T(8,128)S(1)} %get-tuple-element.8.refs_2_), custom_call_target="tpu_custom_call" | custom-call | tf_op jit(solution)/shard_map/pallas_call | solution.py:632

commit v4 on v3

--- a/solution.py
+++ b/solution.py
@@ -20,6 +20,7 @@
 ZPAD = 2
 SXX, SXZ, SXY, SYY, SYZ, SZZ = range(6)
 LAME, SHEAR, BUOY = range(3)
+NEAR_START, WIDE_START, WIDE_SPEED, LATE_SOURCE = range(4)
 STRIP = 10
 KEPT = 4
 REACH = STRIP - KEPT
@@ -79,14 +80,63 @@
     source_wing,
     *rest,
 ):
-    x_send, x_recv, wing_send, wing_recv, corner_recv = (rest[3 * i : 3 * i + 3] for i in range(5))
-    in_sem, hop_send, hop_recv, face_send, face_recv = rest[15:]
+    x_send, x_recv, wing_send, wing_recv, corner_recv = (rest[4 * i : 4 * i + 4] for i in range(5))
+    in_sem, hop_send, hop_recv, face_send, face_recv = rest[20:]
     depth, width = buoy_in.shape[0], buoy_in.shape[1]
     rows = trace.shape[1]
     tiles = n_x * n_y
     gx, gy = lax.axis_index("gx"), lax.axis_index("gy")
     inner = pl.ds(MARGIN, width)
     planes = pl.ds(ZPAD, depth)
+
+    half_x, half_y = n_x // 2, n_y // 2
+    my_a = lax.rem(gx, half_x) * 2 + lax.rem(gy, 2)
+    my_b = (gx // half_x) * half_y + gy // 2
+    size_a, size_b = n_x, n_y
+
+    quarter_y = n_y // 4
+    high_y, low_y = gx // half_x, gy // half_y
+
+    def around_ring(size):
+        return lambda step: -min(step, size - step)
+
+    offsets_a = [(dz, dc) for dz in sorted(range(half_x), key=around_ring(half_x)) for dc in range(2)][:-2] + [(0, 1)]
+    offsets_b = sorted(
+        ((dy, dx) for dy in range(4) for dx in range(quarter_y) if dy + dx > 0),
+        key=lambda step: around_ring(4)(step[0]) + around_ring(quarter_y)(step[1]),
+    )
+
+    def partner_a(i):
+        dz, dc = offsets_a[i]
+        near = lax.rem(lax.rem(gx, half_x) + dz, half_x)
+        core = lax.rem(gy + dc, 2)
+        return near * 2 + core, ((gx // half_x) * half_x + near, (gy // 2) * 2 + core)
+
+    def partner_b(i):
+        dy, dx = offsets_b[i]
+        line = lax.rem(high_y * 2 + low_y + dy, 4)
+        spot = lax.rem(lax.rem(gy, half_y) // 2 + dx, quarter_y)
+        outer = lax.rem(line, 2) * quarter_y + spot
+        return (line // 2) * half_y + outer, (
+            (line // 2) * half_x + lax.rem(gx, half_x),
+            outer * 2 + lax.rem(gy, 2),
+        )
+
+    up_x = (lax.rem(gx + 1, n_x), gy)
+    down_x = (lax.rem(gx + n_x - 1, n_x), gy)
+    up_y = (gx, lax.rem(gy + 1, n_y))
+    down_y = (gx, lax.rem(gy + n_y - 1, n_y))
+    corners = tuple((x, y) for x in (down_x[0], up_x[0]) for y in (down_y[1], up_y[1]))
+    around = (down_x, up_x, down_y, up_y) + corners
+
+    barrier = pltpu.get_barrier_semaphore()
+
+    partners_a = [partner_a(i) for i in range(size_a - 1)]
+    partners_b = [partner_b(i) for i in range(size_b - 1)]
+    for _, target in partners_a + partners_b:
+        pl.semaphore_signal(barrier, inc=1, device_id=target, device_id_type=MESH)
+    for target in around:
+        pl.semaphore_signal(barrier, inc=1, device_id=target, device_id_type=MESH)
 
     loads = [
         pltpu.make_async_copy(src, dst, in_sem.at[i])
@@ -109,37 +159,6 @@
     for load in loads:
         load.start()
 
-    half_x, half_y = n_x // 2, n_y // 2
-    my_a = lax.rem(gx, half_x) * 2 + lax.rem(gy, 2)
-    my_b = (gx // half_x) * half_y + gy // 2
-    size_a, size_b = n_x, n_y
-
-    def at_a(a):
-        return ((gx // half_x) * half_x + a // 2, (gy // 2) * 2 + lax.rem(a, 2))
-
-    def at_b(b):
-        return ((b // half_y) * half_x + lax.rem(gx, half_x), lax.rem(b, half_y) * 2 + lax.rem(gy, 2))
-
-    up_x = (lax.rem(gx + 1, n_x), gy)
-    down_x = (lax.rem(gx + n_x - 1, n_x), gy)
-    up_y = (gx, lax.rem(gy + 1, n_y))
-    down_y = (gx, lax.rem(gy + n_y - 1, n_y))
-    corners = tuple((x, y) for x in (down_x[0], up_x[0]) for y in (down_y[1], up_y[1]))
-    around = (down_x, up_x, down_y, up_y) + corners
-
-    barrier = pltpu.get_barrier_semaphore()
-
-    def greet(place, me, size):
-        def run(i, _):
-            pl.semaphore_signal(barrier, inc=1, device_id=place(lax.rem(me + i, size)), device_id_type=MESH)
-            return 0
-
-        lax.fori_loop(1, size, run, 0)
-
-    greet(at_a, my_a, size_a)
-    greet(at_b, my_b, size_b)
-    for target in around:
-        pl.semaphore_signal(barrier, inc=1, device_id=target, device_id_type=MESH)
 
     blank = jnp.zeros((ZPAD, width + 2 * MARGIN, LANES), jnp.float32)
     for ref, comps in ((speed, (0, 1, 2)), (tension, (SXZ, SYZ, SZZ))):
@@ -184,6 +203,9 @@
     from_down = (lane_row >= WINGS) & (turn < REACH)
     below = MARGIN + width
 
+    def has_corners(e):
+        return e in (WIDE_SPEED, WIDE_START)
+
     def face_copies(e):
         strips = x_send[e].shape[1]
         count = wing_send[e].shape[0]
@@ -194,7 +216,7 @@
             (wing_send[e], wing_recv[e].at[0], down_y),
             (wing_send[e], wing_recv[e].at[1], up_y),
         ]
-        if e < 2:
+        if has_corners(e):
             for k, target in enumerate(corners):
                 moves.append((x_send[e].at[k // 2, tail], corner_recv[e].at[k // 2, k % 2], target))
         return [
@@ -209,13 +231,18 @@
             for k, (src, dst, target) in enumerate(moves)
         ]
 
-    def pack_faces(e, fields):
+    def pack_faces(e, x_fields, wing_fields):
         reach = x_send[e].shape[2]
-        for i, (ref, comp, first) in enumerate(fields):
-            def strip(z, heap, i=i, ref=ref, comp=comp, first=first):
-                plane = ref[comp, z + first, inner, :]
+        for i, (ref, comp, first) in enumerate(x_fields):
+            def rows_of(z, _, i=i, ref=ref, comp=comp, first=first):
                 x_send[e][0, i * depth + z] = ref[comp, z + first, pl.ds(MARGIN, reach), :]
                 x_send[e][1, i * depth + z] = ref[comp, z + first, pl.ds(below - reach, reach), :]
+                return 0
+
+            lax.fori_loop(0, depth, rows_of, 0, unroll=True)
+        for i, (ref, comp, first) in enumerate(wing_fields):
+            def strip(z, heap, ref=ref, comp=comp, first=first):
+                plane = ref[comp, z + first, inner, :]
                 start = z * STRIP
                 low, high = heap
                 low = jnp.where(lane_row >= start, pltpu.roll(plane, start + KEPT, 1), low)
@@ -226,13 +253,15 @@
             low, high = lax.fori_loop(0, depth, strip, (empty, empty), unroll=True)
             wing = jnp.where(lane_row >= WINGS, high, low)
             wing_send[e][i] = wing
-            if e < 2:
-                x_send[e][0, len(fields) * depth + i] = wing[:reach]
-                x_send[e][1, len(fields) * depth + i] = wing[width - reach :]
+            if has_corners(e):
+                x_send[e][0, len(x_fields) * depth + i] = wing[:reach]
+                x_send[e][1, len(x_fields) * depth + i] = wing[width - reach :]
+
+    def send_faces(e):
         for copy in face_copies(e):
             copy.start()
 
-    def take_faces(e, fields):
+    def take_faces(e, x_fields, wing_fields):
         reach = x_send[e].shape[2]
         for copy in face_copies(e):
             copy.wait_recv()
@@ -244,7 +273,7 @@
                     ref[...] = jnp.zeros(ref.shape, jnp.float32)
 
         corner = corner_recv[e]
-        both = e < 2
+        both = has_corners(e)
         clear(gy == n_y - 1, wing_recv[e].at[0], *([corner.at[0, 0], corner.at[1, 0]] if both else []))
         clear(gy == 0, wing_recv[e].at[1], *([corner.at[0, 1], corner.at[1, 1]] if both else []))
         clear(gx == n_x - 1, x_recv[e].at[0], *([corner.at[0]] if both else []))
@@ -253,18 +282,19 @@
         def mixed(up, down, own):
             return jnp.where(from_up, up, jnp.where(from_down, down, own))
 
-        for i, (ref, comp, first, wing, at) in enumerate(fields):
+        for i, (ref, comp, first) in enumerate(x_fields):
             def rows_of(z, _, i=i, ref=ref, comp=comp, first=first):
                 ref[comp, z + first, pl.ds(below, reach), :] = x_recv[e][0, i * depth + z]
                 ref[comp, z + first, pl.ds(MARGIN - reach, reach), :] = x_recv[e][1, i * depth + z]
                 return 0
 
             lax.fori_loop(0, depth, rows_of, 0, unroll=True)
+        for i, (wing, at) in enumerate(wing_fields):
             wing[at, inner, :] = mixed(wing_recv[e][0, i], wing_recv[e][1, i], wing_send[e][i])
             if both:
                 for side, start in ((0, below), (1, MARGIN - reach)):
                     wing[at, pl.ds(start, reach), :] = mixed(
-                        corner[side, 0, i], corner[side, 1, i], x_recv[e][side, len(fields) * depth + i]
+                        corner[side, 0, i], corner[side, 1, i], x_recv[e][side, len(x_fields) * depth + i]
                     )
 
     def difference(at, upward):
@@ -417,65 +447,52 @@
             for comp, change in changes(strained, solid_wing[LAME, near_at, :], solid_wing[SHEAR, near_at, :]):
                 tension_wing[comp, near_at, :] = tension_wing[comp, near_at, :] + change
 
+    loads[3].wait()
+    near_x, near_y = (SXX, SXZ, SXY), (SXY, SYY, SYZ)
+    near_fields = [(tension, comp, ZPAD) for comp in near_x]
+    near_wings = [(tension_wing, comp) for comp in near_y]
+    pack_faces(NEAR_START, near_fields, [(tension, comp, ZPAD) for comp in near_y])
     pl.semaphore_wait(barrier, size_a + size_b - 2 + len(around))
 
     def hop_a(i):
-        to = lax.rem(my_a + i, size_a)
+        to, target = partners_a[i]
         return pltpu.make_async_remote_copy(
             src_ref=packed.at[to],
             dst_ref=first_hop.at[lax.rem(my_a, CAP), :, my_a // CAP],
-            send_sem=hop_send.at[0, i],
-            recv_sem=hop_recv.at[0, i],
-            device_id=at_a(to),
+            send_sem=hop_send.at[0, i + 1],
+            recv_sem=hop_recv.at[0, i + 1],
+            device_id=target,
             device_id_type=MESH,
         )
 
     def hop_b(i):
-        to = lax.rem(my_b + i, size_b)
+        to, target = partners_b[i]
         return pltpu.make_async_remote_copy(
             src_ref=regrouped.at[to // CAP, lax.rem(to, CAP)],
             dst_ref=second_hop.at[my_b],
-            send_sem=hop_send.at[1, i],
-            recv_sem=hop_recv.at[1, i],
-            device_id=at_b(to),
+            send_sem=hop_send.at[1, i + 1],
+            recv_sem=hop_recv.at[1, i + 1],
+            device_id=target,
             device_id_type=MESH,
         )
 
-    def start(make):
-        def run(i, _):
-            make(i).start()
-            return 0
-
-        return run
-
-    def landed(make):
-        def run(i, _):
-            make(i).wait_recv()
-            return 0
-
-        return run
-
-    def sent(make):
-        def run(i, _):
-            make(i).wait_send()
-            return 0
-
-        return run
-
-    lax.fori_loop(1, size_a, start(hop_a), 0)
+    hops_a = [hop_a(i) for i in range(size_a - 1)]
+    hops_b = [hop_b(i) for i in range(size_b - 1)]
+    for copy in hops_a:
+        copy.start()
     own_a = pltpu.make_async_copy(
         packed.at[my_a], first_hop.at[lax.rem(my_a, CAP), :, my_a // CAP], hop_recv.at[0, 0]
     )
     own_a.start()
-    start_fields = [(tension, comp, ZPAD, tension_wing, comp) for comp in range(6)]
-    start_fields += [(solid, comp, 0, solid_wing, comp) for comp in range(3)]
-    speed_fields = [(speed, comp, ZPAD, speed_wing, comp) for comp in range(3)]
-    late_fields = [(source, 3 + comp, 0, source_wing, comp) for comp in range(3)]
-    for load in (loads[3], *loads[5:8]):
+    send_faces(NEAR_START)
+    for load in loads[5:8]:
         load.wait()
-    pack_faces(0, [field[:3] for field in start_fields])
+    wide_fields = [(tension, comp, ZPAD) for comp in range(6)] + [(solid, comp, 0) for comp in range(3)]
+    wide_wings = [(tension_wing, comp) for comp in range(6)] + [(solid_wing, comp) for comp in range(3)]
+    pack_faces(WIDE_START, wide_fields, wide_fields)
     own_a.wait()
-    lax.fori_loop(1, size_a, landed(hop_a), 0)
+    for copy in reversed(hops_a):
+        copy.wait_recv()
     heaps = [first_hop[p].reshape(lines // CAP, LANES) for p in range(CAP)]
     span = CAP * FEATURES
     lane_hop = lax.broadcasted_iota(jnp.int32, (lines // CAP, LANES), 1)
@@ -486,18 +503,21 @@
             turned = heaps[p] if shift == 0 else pltpu.roll(heaps[p], shift, 1)
             merged = turned if p == 0 else jnp.where(lane_hop >= span * p, turned, merged)
         regrouped[:, low] = merged.reshape(size_b // CAP, size_a // CAP, 1, LANES)
-    lax.fori_loop(1, size_b, start(hop_b), 0)
+    for copy in hops_b:
+        copy.start()
     own_b = pltpu.make_async_copy(
         regrouped.at[my_b // CAP, lax.rem(my_b, CAP)], second_hop.at[my_b], hop_recv.at[1, 0]
     )
     own_b.start()
 
-    take_faces(0, start_fields)
+    send_faces(WIDE_START)
+    take_faces(NEAR_START, near_fields, near_wings)
     loads[4].wait()
     push_speed(0, 0, False)
 
     own_b.wait()
-    lax.fori_loop(1, size_b, landed(hop_b), 0)
+    for copy in reversed(hops_b):
+        copy.wait_recv()
     arrived = second_hop[...].reshape(lines, LANES)
     arrived = jnp.concatenate([arrived, pltpu.roll(arrived, LANES // 2, 1)], axis=0).T
     heap = LANES // 2 // FEATURES
@@ -520,19 +540,24 @@
 
     lay_sources(0)
     add_source(0)
-    pack_faces(1, [field[:3] for field in speed_fields])
+    speed_fields = [(speed, comp, ZPAD) for comp in range(3)]
+    pack_faces(WIDE_SPEED, speed_fields, speed_fields)
+    send_faces(WIDE_SPEED)
     lay_sources(1)
-    pack_faces(2, [field[:3] for field in late_fields])
+    late_fields = [(source, 3 + comp, 0) for comp in range(3)]
+    pack_faces(LATE_SOURCE, late_fields, late_fields)
+    send_faces(LATE_SOURCE)
     for load in loads[8:]:
         load.wait()
-    take_faces(1, speed_fields)
+    take_faces(WIDE_START, wide_fields, wide_wings)
+    take_faces(WIDE_SPEED, speed_fields, [(speed_wing, comp) for comp in range(3)])
     push_stress(4, False)
-    take_faces(2, late_fields)
+    take_faces(LATE_SOURCE, late_fields, [(source_wing, comp) for comp in range(3)])
     push_speed(2, 1, True)
     push_stress(0, True)
-    lax.fori_loop(1, size_a, sent(hop_a), 0)
-    lax.fori_loop(1, size_b, sent(hop_b), 0)
-    for e in range(3):
+    for copy in hops_a + hops_b:
+        copy.wait_send()
+    for e in range(4):
         for copy in face_copies(e):
             copy.wait_send()
 
@@ -564,7 +589,7 @@
     depth, width, lanes = buoyancy.shape
     rows = station_trace.shape[0]
     tiles = n_x * n_y
-    exchanges = ((9, 4, 1), (3, 6, 1), (3, 2, 0))
+    exchanges = ((3, 2, 0), (9, 4, 1), (3, 6, 1), (3, 2, 0))
     padded = (depth + 2 * ZPAD, width + 2 * MARGIN, lanes)
     f32, b16 = jnp.float32, jnp.bfloat16
     far = pl.BlockSpec(memory_space=pltpu.HBM)

time: 38.1 us -> 36.1 us (0.948)
  Pallas kernels: 36.7 us -> 34.6 us
    pallas_call x1, Pallas kernels: 35.7 us -> 33.6 us  [body(): pl.pallas_call(functools.partial(kernel, n_x, n_y), out_shape=[pltpu.VMEM...]
where the time goes in v4:
time: 36.1 us; the launch traced here: 35.9 us
  Pallas kernels  34.6 us (96%)
  between operations  1.29 us (4%)
    pallas_call x1, Pallas kernels, body(): pl.pallas_call(functools.partial(kernel, n_x, n_y), out_shape=[pltpu.VMEM...  33.6 us
    pallas_call x1, Pallas kernels, body(): pl.pallas_call(deliver, out_shape=[pltpu.HBM(array.shape, f32) for array...  1.03 us

profile of v4, /device:TPU:1, one launch (start us, length us, event | category | flops | bytes accessed | tf_op | source)
XLA Modules:
  0.0 35.9 jit_solution(1940375973656767656)
XLA Ops:
  1.3 33.6 %shard_map.139 = (f32[3,6,32,128]{3,2,1,0:T(8,128)S(1)}, f32[6,6,32,128]{3,2,1,0:T(8,128)S(1)}, f32[3,6,32,128]{3,2,1,0:T(8,128)S(1)}) custom-call(f32[3,6,32,128]{3,2,1,0:T(8,128)} %vel_in.1, f32[6,6,32,128]{3,2,1,0:T(8,128)} %str_in.1, f32[6,32,128]{2,1,0:T(8,128)} %lame_in.1, f32[6,32,128]{2,1,0:T(8,128)} %shear_in.1, f32[6,32,128]{2,1,0:T(8,128)} %buoy_in.1, ...), custom_call_target="tpu_custom_call" | custom-call | tf_op jit(solution)/shard_map/pallas_call | solution.py:596
  34.9 1.0 %shard_map.140 = (f32[3,6,32,128]{3,2,1,0:T(8,128)}, f32[6,6,32,128]{3,2,1,0:T(8,128)}, f32[3,6,32,128]{3,2,1,0:T(8,128)}) custom-call(f32[3,6,32,128]{3,2,1,0:T(8,128)S(1)} %get-tuple-element.6.refs_0_, f32[6,6,32,128]{3,2,1,0:T(8,128)S(1)} %get-tuple-element.7.refs_1_, f32[3,6,32,128]{3,2,1,0:T(8,128)S(1)} %get-tuple-element.8.refs_2_), custom_call_target="tpu_custom_call" | custom-call | tf_op jit(solution)/shard_map/pallas_call | solution.py:657

commit v5 on v4

--- a/solution.py
+++ b/solution.py
@@ -78,6 +78,9 @@
     tension_wing,
     solid_wing,
     source_wing,
+    band,
+    choice,
+    slopes,
     *rest,
 ):
     x_send, x_recv, wing_send, wing_recv, corner_recv = (rest[4 * i : 4 * i + 4] for i in range(5))
@@ -203,6 +206,65 @@
     from_down = (lane_row >= WINGS) & (turn < REACH)
     below = MARGIN + width
 
+    def by_pieces(parts, matrix):
+        count = parts[0].shape[0]
+        total = jnp.dot(jnp.concatenate(parts, axis=0), matrix, preferred_element_type=jnp.float32)
+        return (total[2 * count :] + total[count : 2 * count]) + total[:count]
+
+    def build_choice():
+        row = lax.broadcasted_iota(jnp.int32, (LANES, LANES), 0)
+        column = lax.broadcasted_iota(jnp.int32, (LANES, LANES), 1)
+        high, low = lax.rem(row + KEPT, LANES), lax.rem(row + REACH, LANES)
+
+        def block(z, _):
+            first = (high < STRIP) & (column == z * STRIP + high)
+            second = (low < STRIP) & (column == WINGS + z * STRIP + low)
+            choice[pl.ds(z * LANES, LANES), :] = (first | second).astype(jnp.float32).astype(jnp.bfloat16)
+            return 0
+
+        lax.fori_loop(0, depth, block, 0, unroll=True)
+
+    def build_band():
+        row = lax.broadcasted_iota(jnp.int32, (LANES, LANES), 0)
+        column = lax.broadcasted_iota(jnp.int32, (LANES, LANES), 1)
+
+        def weights(away, upward):
+            near, far = 24.0 * C_NEAR, -24.0 * C_FAR
+            ahead = away if upward else away + 1
+            value = jnp.where(ahead == 1, near, 0.0) + jnp.where(ahead == 0, -near, 0.0)
+            value = value + jnp.where(ahead == 2, -far, 0.0) + jnp.where(ahead == -1, far, 0.0)
+            return value.astype(jnp.bfloat16)
+
+        for side, upward in enumerate((False, True)):
+            centre = weights(row - column, upward)
+
+            def block(z, _, side=side, upward=upward, centre=centre):
+                band[side, z, pl.ds(0, LANES), :] = centre
+                high = row - z * STRIP
+                low = row - WINGS - z * STRIP
+                place = jnp.where(
+                    (high >= KEPT) & (high < STRIP),
+                    high + LANES - KEPT,
+                    jnp.where((low >= 0) & (low < REACH), low - REACH, 4 * LANES),
+                )
+                band[side, z, pl.ds(LANES, LANES), :] = weights(place - column, upward)
+                return 0
+
+            lax.fori_loop(0, depth, block, 0, unroll=True)
+
+    def take_slopes(ref, wing, fields, start, count):
+        rows_at = pl.ds(start, count)
+        for k, (comp, upward) in enumerate(fields):
+            edge = pieces(wing[comp, rows_at, :])
+
+            def plane(z, _, k=k, comp=comp, upward=upward, edge=edge):
+                core = pieces(ref[comp, z + ZPAD, rows_at, :])
+                both = [jnp.concatenate([a, b], axis=1) for a, b in zip(core, edge)]
+                slopes[k, z, rows_at, :] = by_pieces(both, band[int(upward), z]) * (1.0 / 24.0)
+                return 0
+
+            lax.fori_loop(0, depth, plane, 0, unroll=True)
+
     def has_corners(e):
         return e in (WIDE_SPEED, WIDE_START)
 
@@ -241,17 +303,8 @@
 
             lax.fori_loop(0, depth, rows_of, 0, unroll=True)
         for i, (ref, comp, first) in enumerate(wing_fields):
-            def strip(z, heap, ref=ref, comp=comp, first=first):
-                plane = ref[comp, z + first, inner, :]
-                start = z * STRIP
-                low, high = heap
-                low = jnp.where(lane_row >= start, pltpu.roll(plane, start + KEPT, 1), low)
-                high = jnp.where(lane_row >= WINGS + start, pltpu.roll(plane, WINGS + start + REACH, 1), high)
-                return low, high
-
-            empty = jnp.zeros((width, LANES), jnp.float32)
-            low, high = lax.fori_loop(0, depth, strip, (empty, empty), unroll=True)
-            wing = jnp.where(lane_row >= WINGS, high, low)
+            planes_of = [pieces(ref[comp, z + first, inner, :]) for z in range(depth)]
+            wing = by_pieces([jnp.concatenate([parts[k] for parts in planes_of], axis=1) for k in range(3)], choice[...])
             wing_send[e][i] = wing
             if has_corners(e):
                 x_send[e][0, len(x_fields) * depth + i] = wing[:reach]
@@ -310,22 +363,8 @@
             return difference(lambda o: ref[comp, z + ZPAD, pl.ds(start + o, count), :], upward)
 
         def along_y(ref, comp, upward):
-            wing = (speed_wing if ref is speed else tension_wing)[comp, pl.ds(start, count), :]
-            centre = ref[comp, z + ZPAD, pl.ds(start, count), :]
-            side = jnp.where(
-                lane_row < LANES // 2,
-                pltpu.roll(wing, LANES - KEPT - z * STRIP, 1),
-                pltpu.roll(wing, LANES - REACH - WINGS - z * STRIP, 1),
-            )
-
-            def at(o):
-                if o == 0:
-                    return centre
-                if o > 0:
-                    return pltpu.roll(jnp.where(lane_row < o, side, centre), LANES - o, 1)
-                return pltpu.roll(jnp.where(lane_row >= LANES + o, side, centre), -o, 1)
-
-            return difference(at, upward)
+            del upward
+            return slopes[comp if ref is speed else comp - SXY, z, pl.ds(start, count), :]
 
         return along_x, along_y, along_z
 
@@ -382,8 +421,12 @@
             (SYZ, stiff * gyz),
         )
 
+    def matrix_rows(margin):
+        return (0, width + 2 * MARGIN) if margin > 0 else (MARGIN, width)
+
     def push_speed(margin, step, final):
         start, count = MARGIN - margin, width + 2 * margin
+        take_slopes(tension, tension_wing, ((SXY, False), (SYY, True), (SYZ, False)), *matrix_rows(margin))
         rows_at = pl.ds(start, count)
 
         def plane(z, _):
@@ -417,6 +460,7 @@
 
     def push_stress(margin, final):
         start, count = MARGIN - margin, width + 2 * margin
+        take_slopes(speed, speed_wing, ((0, True), (1, False), (2, True)), *matrix_rows(margin))
         rows_at = pl.ds(start, count)
 
         def plane(z, _):
@@ -447,11 +491,6 @@
             for comp, change in changes(strained, solid_wing[LAME, near_at, :], solid_wing[SHEAR, near_at, :]):
                 tension_wing[comp, near_at, :] = tension_wing[comp, near_at, :] + change
 
-    loads[3].wait()
-    near_x, near_y = (SXX, SXZ, SXY), (SXY, SYY, SYZ)
-    near_fields = [(tension, comp, ZPAD) for comp in near_x]
-    near_wings = [(tension_wing, comp) for comp in near_y]
-    pack_faces(NEAR_START, near_fields, [(tension, comp, ZPAD) for comp in near_y])
     pl.semaphore_wait(barrier, size_a + size_b - 2 + len(around))
 
     def hop_a(i):
@@ -484,7 +523,14 @@
         packed.at[my_a], first_hop.at[lax.rem(my_a, CAP), :, my_a // CAP], hop_recv.at[0, 0]
     )
     own_a.start()
+    build_choice()
+    loads[3].wait()
+    near_x, near_y = (SXX, SXZ, SXY), (SXY, SYY, SYZ)
+    near_fields = [(tension, comp, ZPAD) for comp in near_x]
+    near_wings = [(tension_wing, comp) for comp in near_y]
+    pack_faces(NEAR_START, near_fields, [(tension, comp, ZPAD) for comp in near_y])
     send_faces(NEAR_START)
+    build_band()
     for load in loads[5:8]:
         load.wait()
     wide_fields = [(tension, comp, ZPAD) for comp in range(6)] + [(solid, comp, 0) for comp in range(3)]
@@ -621,6 +667,9 @@
             pltpu.VMEM((depth * width, CAP * tiles), b16),
             pltpu.VMEM((lanes, CAP * tiles), b16),
             *[pltpu.VMEM((fields, *padded[1:]), f32) for fields in (3, 6, 3, 3)],
+            pltpu.VMEM((2, depth, 2 * lanes, lanes), b16),
+            pltpu.VMEM((depth * lanes, lanes), b16),
+            pltpu.VMEM((3, depth, *padded[1:]), f32),
             *[pltpu.VMEM((2, fields * (depth + wings), reach, lanes), f32) for fields, reach, wings in exchanges],
             *[pltpu.VMEM((2, fields * (depth + wings), reach, lanes), f32) for fields, reach, wings in exchanges],
             *[pltpu.VMEM((fields, width, lanes), f32) for fields, reach, wings in exchanges],

time: 36.1 us -> 33.5 us (0.928)
  Pallas kernels: 34.6 us -> 32.1 us
    pallas_call x1, Pallas kernels: 33.6 us -> 31 us  [body(): pl.pallas_call(functools.partial(kernel, n_x, n_y), out_shape=[pltpu.VMEM...]
where the time goes in v5:
time: 33.5 us; the launch traced here: 33.4 us
  Pallas kernels  32.1 us (96%)
  between operations  1.29 us (4%)
    pallas_call x1, Pallas kernels, body(): pl.pallas_call(functools.partial(kernel, n_x, n_y), out_shape=[pltpu.VMEM...  31 us
    pallas_call x1, Pallas kernels, body(): pl.pallas_call(deliver, out_shape=[pltpu.HBM(array.shape, f32) for array...  1.03 us

profile of v5, /device:TPU:1, one launch (start us, length us, event | category | flops | bytes accessed | tf_op | source)
XLA Modules:
  0.0 33.4 jit_solution(4523696275811996287)
XLA Ops:
  1.3 31.0 %shard_map.139 = (f32[3,6,32,128]{3,2,1,0:T(8,128)S(1)}, f32[6,6,32,128]{3,2,1,0:T(8,128)S(1)}, f32[3,6,32,128]{3,2,1,0:T(8,128)S(1)}) custom-call(f32[3,6,32,128]{3,2,1,0:T(8,128)} %vel_in.1, f32[6,6,32,128]{3,2,1,0:T(8,128)} %str_in.1, f32[6,32,128]{2,1,0:T(8,128)} %lame_in.1, f32[6,32,128]{2,1,0:T(8,128)} %shear_in.1, f32[6,32,128]{2,1,0:T(8,128)} %buoy_in.1, ...), custom_call_target="tpu_custom_call" | custom-call | tf_op jit(solution)/shard_map/pallas_call | solution.py:642
  32.3 1.0 %shard_map.140 = (f32[3,6,32,128]{3,2,1,0:T(8,128)}, f32[6,6,32,128]{3,2,1,0:T(8,128)}, f32[3,6,32,128]{3,2,1,0:T(8,128)}) custom-call(f32[3,6,32,128]{3,2,1,0:T(8,128)S(1)} %get-tuple-element.6.refs_0_, f32[6,6,32,128]{3,2,1,0:T(8,128)S(1)} %get-tuple-element.7.refs_1_, f32[3,6,32,128]{3,2,1,0:T(8,128)S(1)} %get-tuple-element.8.refs_2_), custom_call_target="tpu_custom_call" | custom-call | tf_op jit(solution)/shard_map/pallas_call | solution.py:706

commit v6 on v5

--- a/solution.py
+++ b/solution.py
@@ -130,6 +130,8 @@
     up_y = (gx, lax.rem(gy + 1, n_y))
     down_y = (gx, lax.rem(gy + n_y - 1, n_y))
     corners = tuple((x, y) for x in (down_x[0], up_x[0]) for y in (down_y[1], up_y[1]))
+    can_down_x, can_up_x = gx > 0, gx < n_x - 1
+    can_down_y, can_up_y = gy > 0, gy < n_y - 1
     around = (down_x, up_x, down_y, up_y) + corners
 
     barrier = pltpu.get_barrier_semaphore()
@@ -273,25 +275,37 @@
         count = wing_send[e].shape[0]
         tail = pl.ds(strips - count, count)
         moves = [
-            (x_send[e].at[0], x_recv[e].at[0], down_x),
-            (x_send[e].at[1], x_recv[e].at[1], up_x),
-            (wing_send[e], wing_recv[e].at[0], down_y),
-            (wing_send[e], wing_recv[e].at[1], up_y),
+            (x_send[e].at[0], x_recv[e].at[0], down_x, can_down_x, can_up_x),
+            (x_send[e].at[1], x_recv[e].at[1], up_x, can_up_x, can_down_x),
+            (wing_send[e], wing_recv[e].at[0], down_y, can_down_y, can_up_y),
+            (wing_send[e], wing_recv[e].at[1], up_y, can_up_y, can_down_y),
         ]
         if has_corners(e):
             for k, target in enumerate(corners):
-                moves.append((x_send[e].at[k // 2, tail], corner_recv[e].at[k // 2, k % 2], target))
+                to_x, from_x = ((can_down_x, can_up_x), (can_up_x, can_down_x))[k // 2]
+                to_y, from_y = ((can_down_y, can_up_y), (can_up_y, can_down_y))[k % 2]
+                moves.append(
+                    (x_send[e].at[k // 2, tail], corner_recv[e].at[k // 2, k % 2], target, to_x & to_y, from_x & from_y)
+                )
         return [
-            pltpu.make_async_remote_copy(
-                src_ref=src,
-                dst_ref=dst,
-                send_sem=face_send.at[e, k],
-                recv_sem=face_recv.at[e, k],
-                device_id=target,
-                device_id_type=MESH,
+            (
+                pltpu.make_async_remote_copy(
+                    src_ref=src,
+                    dst_ref=dst,
+                    send_sem=face_send.at[e, k],
+                    recv_sem=face_recv.at[e, k],
+                    device_id=target,
+                    device_id_type=MESH,
+                ),
+                sends,
+                takes,
             )
-            for k, (src, dst, target) in enumerate(moves)
+            for k, (src, dst, target, sends, takes) in enumerate(moves)
         ]
+
+    def sent_faces(e):
+        for copy, sends, _ in face_copies(e):
+            pl.when(sends)(copy.wait_send)
 
     def pack_faces(e, x_fields, wing_fields):
         reach = x_send[e].shape[2]
@@ -311,13 +325,13 @@
                 x_send[e][1, len(x_fields) * depth + i] = wing[width - reach :]
 
     def send_faces(e):
-        for copy in face_copies(e):
-            copy.start()
+        for copy, sends, _ in face_copies(e):
+            pl.when(sends)(copy.start)
 
     def take_faces(e, x_fields, wing_fields):
         reach = x_send[e].shape[2]
-        for copy in face_copies(e):
-            copy.wait_recv()
+        for copy, _, takes in face_copies(e):
+            pl.when(takes)(copy.wait_recv)
 
         def clear(at_edge, *refs):
             @pl.when(at_edge)
@@ -596,16 +610,16 @@
     for load in loads[8:]:
         load.wait()
     take_faces(WIDE_START, wide_fields, wide_wings)
+    for copy in hops_a + hops_b:
+        copy.wait_send()
+    for e in (NEAR_START, WIDE_START, WIDE_SPEED):
+        sent_faces(e)
     take_faces(WIDE_SPEED, speed_fields, [(speed_wing, comp) for comp in range(3)])
     push_stress(4, False)
+    sent_faces(LATE_SOURCE)
     take_faces(LATE_SOURCE, late_fields, [(source_wing, comp) for comp in range(3)])
     push_speed(2, 1, True)
     push_stress(0, True)
-    for copy in hops_a + hops_b:
-        copy.wait_send()
-    for e in range(4):
-        for copy in face_copies(e):
-            copy.wait_send()
 
 
 def deliver(*refs):

time: 33.5 us -> 31.2 us (0.931)
  the two profiles are of different devices: /device:TPU:1 before, /device:TPU:17 now
where the time goes in v6:
time: 31.2 us; the launch traced here: 31 us
  Pallas kernels  29.7 us (95%)
  between operations  1.29 us (4%)
    pallas_call x1, Pallas kernels, body(): pl.pallas_call(functools.partial(kernel, n_x, n_y), out_shape=[pltpu.VMEM...  28.7 us
    pallas_call x1, Pallas kernels, body(): pl.pallas_call(deliver, out_shape=[pltpu.HBM(array.shape, f32) for array...  1.03 us

profile of v6, /device:TPU:17, one launch (start us, length us, event | category | flops | bytes accessed | tf_op | source)
XLA Modules:
  0.0 31.0 jit_solution(7651080935808062189)
XLA Ops:
  1.3 28.7 %shard_map.139 = (f32[3,6,32,128]{3,2,1,0:T(8,128)S(1)}, f32[6,6,32,128]{3,2,1,0:T(8,128)S(1)}, f32[3,6,32,128]{3,2,1,0:T(8,128)S(1)}) custom-call(f32[3,6,32,128]{3,2,1,0:T(8,128)} %vel_in.1, f32[6,6,32,128]{3,2,1,0:T(8,128)} %str_in.1, f32[6,32,128]{2,1,0:T(8,128)} %lame_in.1, f32[6,32,128]{2,1,0:T(8,128)} %shear_in.1, f32[6,32,128]{2,1,0:T(8,128)} %buoy_in.1, ...), custom_call_target="tpu_custom_call" | custom-call | tf_op jit(solution)/shard_map/pallas_call | solution.py:656
  29.9 1.0 %shard_map.140 = (f32[3,6,32,128]{3,2,1,0:T(8,128)}, f32[6,6,32,128]{3,2,1,0:T(8,128)}, f32[3,6,32,128]{3,2,1,0:T(8,128)}) custom-call(f32[3,6,32,128]{3,2,1,0:T(8,128)S(1)} %get-tuple-element.6.refs_0_, f32[6,6,32,128]{3,2,1,0:T(8,128)S(1)} %get-tuple-element.7.refs_1_, f32[3,6,32,128]{3,2,1,0:T(8,128)S(1)} %get-tuple-element.8.refs_2_), custom_call_target="tpu_custom_call" | custom-call | tf_op jit(solution)/shard_map/pallas_call | solution.py:720

commit v7 on v6

--- a/solution.py
+++ b/solution.py
@@ -37,6 +37,26 @@
 
 def dot_nt(left, right):
     return lax.dot_general(left, right, (((1,), (1,)), ((), ())), preferred_element_type=jnp.float32)
+
+
+def difference(at, upward):
+    if upward:
+        return C_NEAR * (at(1) - at(0)) + C_FAR * (at(2) - at(-1))
+    return C_NEAR * (at(0) - at(-1)) + C_FAR * (at(1) - at(-2))
+
+
+def changes(strained, lame, shear):
+    exx, eyy, ezz, gxy, gxz, gyz = strained
+    stiff = STEP_DT * shear
+    common = STEP_DT * lame * (exx + eyy + ezz)
+    return (
+        (SXX, common + 2.0 * stiff * exx),
+        (SYY, common + 2.0 * stiff * eyy),
+        (SZZ, common + 2.0 * stiff * ezz),
+        (SXY, stiff * gxy),
+        (SXZ, stiff * gxz),
+        (SYZ, stiff * gyz),
+    )
 
 
 def kernel(
@@ -54,15 +74,13 @@
     tile_in,
     cell_in,
     count,
-    vel_out,
-    str_out,
-    kern_out,
     speed,
     tension,
     solid,
     strain,
     accel,
     kern,
+    slopes,
     trace,
     tile,
     cell,
@@ -80,7 +98,6 @@
     source_wing,
     band,
     choice,
-    slopes,
     *rest,
 ):
     x_send, x_recv, wing_send, wing_recv, corner_recv = (rest[4 * i : 4 * i + 4] for i in range(5))
@@ -364,11 +381,6 @@
                         corner[side, 0, i], corner[side, 1, i], x_recv[e][side, len(x_fields) * depth + i]
                     )
 
-    def difference(at, upward):
-        if upward:
-            return C_NEAR * (at(1) - at(0)) + C_FAR * (at(2) - at(-1))
-        return C_NEAR * (at(0) - at(-1)) + C_FAR * (at(1) - at(-2))
-
     def tile_part(z, start, count):
         def along_z(ref, comp, upward):
             return difference(lambda o: ref[comp, z + ZPAD + o, pl.ds(start, count), :], upward)
@@ -422,23 +434,10 @@
         gyz = along_z(speed, 1, True) + along_y(speed, 2, True)
         return exx, eyy, ezz, gxy, gxz, gyz
 
-    def changes(strained, lame, shear):
-        exx, eyy, ezz, gxy, gxz, gyz = strained
-        stiff = STEP_DT * shear
-        common = STEP_DT * lame * (exx + eyy + ezz)
-        return (
-            (SXX, common + 2.0 * stiff * exx),
-            (SYY, common + 2.0 * stiff * eyy),
-            (SZZ, common + 2.0 * stiff * ezz),
-            (SXY, stiff * gxy),
-            (SXZ, stiff * gxz),
-            (SYZ, stiff * gyz),
-        )
-
     def matrix_rows(margin):
         return (0, width + 2 * MARGIN) if margin > 0 else (MARGIN, width)
 
-    def push_speed(margin, step, final):
+    def push_speed(margin, step):
         start, count = MARGIN - margin, width + 2 * margin
         take_slopes(tension, tension_wing, ((SXY, False), (SYY, True), (SYZ, False)), *matrix_rows(margin))
         rows_at = pl.ds(start, count)
@@ -450,8 +449,6 @@
                     rate = rate + source[3 * step + k, z, rows_at, :]
                 value = speed[k, z + ZPAD, rows_at, :] + factor * rate
                 speed[k, z + ZPAD, rows_at, :] = value
-                if final:
-                    vel_out[k, z] = value[margin : margin + width]
             return 0
 
         lax.fori_loop(0, depth, plane, 0, unroll=True)
@@ -472,7 +469,7 @@
 
         lax.fori_loop(0, depth, plane, 0, unroll=True)
 
-    def push_stress(margin, final):
+    def push_stress(margin):
         start, count = MARGIN - margin, width + 2 * margin
         take_slopes(speed, speed_wing, ((0, True), (1, False), (2, True)), *matrix_rows(margin))
         rows_at = pl.ds(start, count)
@@ -481,20 +478,7 @@
             strained = strains(*tile_part(z, start, count))
             for comp, change in changes(strained, solid[LAME, z, rows_at, :], solid[SHEAR, z, rows_at, :]):
                 value = tension[comp, z + ZPAD, rows_at, :] + change
-                if final:
-                    str_out[comp, z] = value
-                else:
-                    tension[comp, z + ZPAD, rows_at, :] = value
-            if final:
-                exx, eyy, ezz, gxy, gxz, gyz = strained
-                f = [strain[comp, z].astype(jnp.float32) for comp in range(6)]
-                a = [accel[comp, z].astype(jnp.float32) for comp in range(3)]
-                v = [speed[comp, z + ZPAD, inner, :] for comp in range(3)]
-                kern_out[0, z] = kern[0, z] - STEP_DT * (f[SXX] + f[SYY] + f[SZZ]) * (exx + eyy + ezz)
-                kern_out[1, z] = kern[1, z] - 2.0 * STEP_DT * (
-                    f[SXX] * exx + f[SYY] * eyy + f[SZZ] * ezz + f[SXY] * gxy + f[SXZ] * gxz + f[SYZ] * gyz
-                )
-                kern_out[2, z] = kern[2, z] - STEP_DT * (a[0] * v[0] + a[1] * v[1] + a[2] * v[2])
+                tension[comp, z + ZPAD, rows_at, :] = value
             return 0
 
         lax.fori_loop(0, depth, plane, 0, unroll=True)
@@ -573,7 +557,7 @@
     send_faces(WIDE_START)
     take_faces(NEAR_START, near_fields, near_wings)
     loads[4].wait()
-    push_speed(0, 0, False)
+    push_speed(0, 0)
 
     own_b.wait()
     for copy in reversed(hops_b):
@@ -615,18 +599,47 @@
     for e in (NEAR_START, WIDE_START, WIDE_SPEED):
         sent_faces(e)
     take_faces(WIDE_SPEED, speed_fields, [(speed_wing, comp) for comp in range(3)])
-    push_stress(4, False)
+    push_stress(4)
     sent_faces(LATE_SOURCE)
     take_faces(LATE_SOURCE, late_fields, [(source_wing, comp) for comp in range(3)])
-    push_speed(2, 1, True)
-    push_stress(0, True)
-
-
-def deliver(*refs):
-    sources, targets, sems = refs[:3], refs[3:6], refs[6]
-    copies = [pltpu.make_async_copy(src, dst, sems.at[i]) for i, (src, dst) in enumerate(zip(sources, targets))]
-    for copy in copies:
-        copy.start()
+    push_speed(2, 1)
+    take_slopes(speed, speed_wing, ((0, True), (1, False), (2, True)), *matrix_rows(0))
+
+
+def finish(speed, tension, solid, strain, accel, kern, slopes, vel_out, str_out, kern_out, str_new, kern_new, vel_sem, plane_sem):
+    depth, width = kern.shape[1], kern.shape[2]
+    inner = pl.ds(MARGIN, width)
+    speed_copy = pltpu.make_async_copy(speed.at[:, pl.ds(ZPAD, depth), inner, :], vel_out, vel_sem.at[0])
+    speed_copy.start()
+    copies = []
+    for z in range(depth):
+
+        def along_z(comp, upward, z=z):
+            return difference(lambda o: speed[comp, z + ZPAD + o, inner, :], upward)
+
+        def along_x(comp, upward, z=z):
+            return difference(lambda o: speed[comp, z + ZPAD, pl.ds(MARGIN + o, width), :], upward)
+
+        exx, eyy, ezz = along_x(0, False), slopes[1, z, inner, :], along_z(2, False)
+        gxy = slopes[0, z, inner, :] + along_x(1, True)
+        gxz = along_z(0, True) + along_x(2, True)
+        gyz = along_z(1, True) + slopes[2, z, inner, :]
+        strained = (exx, eyy, ezz, gxy, gxz, gyz)
+        for comp, change in changes(strained, solid[LAME, z, inner, :], solid[SHEAR, z, inner, :]):
+            str_new[comp, z] = tension[comp, z + ZPAD, inner, :] + change
+        f = [strain[comp, z].astype(jnp.float32) for comp in range(6)]
+        a = [accel[comp, z].astype(jnp.float32) for comp in range(3)]
+        v = [speed[comp, z + ZPAD, inner, :] for comp in range(3)]
+        kern_new[0, z] = kern[0, z] - STEP_DT * (f[SXX] + f[SYY] + f[SZZ]) * (exx + eyy + ezz)
+        kern_new[1, z] = kern[1, z] - 2.0 * STEP_DT * (
+            f[SXX] * exx + f[SYY] * eyy + f[SZZ] * ezz + f[SXY] * gxy + f[SXZ] * gxz + f[SYZ] * gyz
+        )
+        kern_new[2, z] = kern[2, z] - STEP_DT * (a[0] * v[0] + a[1] * v[1] + a[2] * v[2])
+        copies.append(pltpu.make_async_copy(str_new.at[:, z], str_out.at[:, z], plane_sem.at[0, z]))
+        copies.append(pltpu.make_async_copy(kern_new.at[:, z], kern_out.at[:, z], plane_sem.at[1, z]))
+        for copy in copies[-2:]:
+            copy.start()
+    speed_copy.wait()
     for copy in copies:
         copy.wait()
 
@@ -656,19 +669,17 @@
     results = pl.pallas_call(
         functools.partial(kernel, n_x, n_y),
         out_shape=[
-            pltpu.VMEM(velocity.shape, f32),
-            pltpu.VMEM(stress.shape, f32),
-            pltpu.VMEM(kernels.shape, f32),
-        ],
-        in_specs=[far] * 11 + [pl.BlockSpec(memory_space=pltpu.SMEM)],
-        out_specs=[pl.BlockSpec(memory_space=pltpu.VMEM)] * 3,
-        scratch_shapes=[
             pltpu.VMEM((3, *padded), f32),
             pltpu.VMEM((6, *padded), f32),
             pltpu.VMEM((3, depth, *padded[1:]), f32),
             pltpu.VMEM(fwd_strain.shape, b16),
             pltpu.VMEM(fwd_accel.shape, b16),
             pltpu.VMEM(kernels.shape, f32),
+            pltpu.VMEM((3, depth, *padded[1:]), f32),
+        ],
+        in_specs=[far] * 11 + [pl.BlockSpec(memory_space=pltpu.SMEM)],
+        out_specs=[pl.BlockSpec(memory_space=pltpu.VMEM)] * 7,
+        scratch_shapes=[
             pltpu.VMEM(station_trace.shape[::-1], f32),
             pltpu.VMEM((1, rows), jnp.int32),
             pltpu.VMEM((1, rows), jnp.int32),
@@ -683,7 +694,6 @@
             *[pltpu.VMEM((fields, *padded[1:]), f32) for fields in (3, 6, 3, 3)],
             pltpu.VMEM((2, depth, 2 * lanes, lanes), b16),
             pltpu.VMEM((depth * lanes, lanes), b16),
-            pltpu.VMEM((3, depth, *padded[1:]), f32),
             *[pltpu.VMEM((2, fields * (depth + wings), reach, lanes), f32) for fields, reach, wings in exchanges],
             *[pltpu.VMEM((2, fields * (depth + wings), reach, lanes), f32) for fields, reach, wings in exchanges],
             *[pltpu.VMEM((fields, width, lanes), f32) for fields, reach, wings in exchanges],
@@ -696,7 +706,7 @@
             pltpu.SemaphoreType.DMA((len(exchanges), 8)),
         ],
         compiler_params=pltpu.CompilerParams(
-            collective_id=0, has_side_effects=True, vmem_limit_bytes=48 * 1024 * 1024
+            collective_id=0, has_side_effects=True, vmem_limit_bytes=32 * 1024 * 1024
         ),
     )(
         *(
@@ -718,11 +728,17 @@
         station_count,
     )
     return pl.pallas_call(
-        deliver,
+        finish,
         out_shape=[pltpu.HBM(array.shape, f32) for array in (velocity, stress, kernels)],
-        in_specs=[pl.BlockSpec(memory_space=pltpu.VMEM)] * 3,
+        in_specs=[pl.BlockSpec(memory_space=pltpu.VMEM)] * 7,
         out_specs=[far] * 3,
-        scratch_shapes=[pltpu.SemaphoreType.DMA((3,))],
+        scratch_shapes=[
+            pltpu.VMEM(stress.shape, f32),
+            pltpu.VMEM(kernels.shape, f32),
+            pltpu.SemaphoreType.DMA((1,)),
+            pltpu.SemaphoreType.DMA((2, depth)),
+        ],
+        compiler_params=pltpu.CompilerParams(vmem_limit_bytes=16 * 1024 * 1024),
     )(*(pltpu.with_memory_space_constraint(array, pltpu.VMEM) for array in results))
 
 

time: 31.2 us -> 31 us (level)
  no operation moved by 1% of the time
where the time goes in v7:
time: 31 us; the launch traced here: 30.8 us
  Pallas kernels  29.5 us (95%)
  between operations  1.29 us (4%)
    pallas_call x1, Pallas kernels, body(): pl.pallas_call(functools.partial(kernel, n_x, n_y), out_shape=[pltpu.VMEM...  28.4 us
    pallas_call x1, Pallas kernels, body(): pl.pallas_call(finish, out_shape=[pltpu.HBM(array.shape, f32) for array i...  1.11 us

profile of v7, /device:TPU:17, one launch (start us, length us, event | category | flops | bytes accessed | tf_op | source)
XLA Modules:
  0.0 30.8 jit_solution(12925258918428486022)
XLA Ops:
  1.3 28.4 %shard_map.139 = (f32[3,10,48,128]{3,2,1,0:T(8,128)S(1)}, f32[6,10,48,128]{3,2,1,0:T(8,128)S(1)}, f32[3,6,48,128]{3,2,1,0:T(8,128)S(1)}, bf16[6,6,32,128]{3,2,1,...) custom-call(f32[3,6,32,128]{3,2,1,0:T(8,128)} %vel_in.1, ...), custom_call_target="tpu_custom_call" | custom-call | tf_op jit(solution)/shard_map/pallas_call | solution.py:669
  29.7 1.1 %shard_map.140 = (f32[3,6,32,128]{3,2,1,0:T(8,128)}, f32[6,6,32,128]{3,2,1,0:T(8,128)}, f32[3,6,32,128]{3,2,1,0:T(8,128)}) custom-call(f32[3,10,48,128]{3,2,1,0:T(8,128)S(1)} %get-tuple-element.10.speed, f32[6,10,48,128]{3,2,1,0:T(8,128)S(1)} %get-tuple-element.11.tension, f32[3,6,48,128]{3,2,1,0:T(8,128)S(1)} %get-tuple-element.12.solid, ...), custom_call_target="tpu_custom_call" | custom-call | tf_op jit(solution)/shard_map/pallas_call | solution.py:730
